TPU v7x, 256 devices: a whole 4x4x8 slice. The times are simulated.
256 devices in a mesh: blk: 16 (over z, y_hi), tp: 4 (over y_lo, core), enc: 4 (over x).
Axes of the slice: x: 4, y: 4 (y_hi: 2, y_lo: 2; y = y_hi * 2 + y_lo), z: 8, core: 2. Of those that a mesh axis runs over, the one named last changes fastest.
Arguments:
- self_query_columns: bfloat16 [8192, 4096], P('blk', ('tp', 'enc')), may hold values from -12 to 12
- text_key_value: bfloat16 [8192, 2, 512], P('blk', None, 'tp'), may hold values from -9 to 9
- cross_query_columns: bfloat16 [8192, 4096], P('blk', ('tp', 'enc')), may hold values from -12 to 12
- image_kv: bfloat16 [16, 2, 6404, 512], P('blk', None, 'enc', 'tp'), may hold values from -9 to 9
- block_images: int32 [64, 16], P('blk'), may hold values from 0 to 1, as said below
- image_owner: int32 [16], replicated, may hold values from 0 to 15, each once
Outputs:
- self_out: bfloat16 [8192, 4096], P('blk', ('tp', 'enc'))
- cross_out: bfloat16 [8192, 4096], P('blk', ('tp', 'enc'))
Inputs may be any that keep to these rules, and one draw needn't show every extreme that they name: `block_images`: each block of 128 text tokens sees one or two images: the image most recently placed before it and, in some blocks, the image placed before that one. Image ids rise along the text, every image is seen by some block, and some block sees two. A permutation: image i's keys and values are slot image_owner[i] of image_kv.
All inputs are finite; a program needn't handle non-finite values.
Results may differ from a plain program's by a relative error of at most 0.007.
Values may be sent and summed in bfloat16 or wider, within the bound.
A program may use at most 64 MiB of HBM per device.

v0:
```python
import math

import jax
import jax.numpy as jnp
from jax import lax
from jax.sharding import PartitionSpec as P

HEAD_SIZE = 128
MASK_BLOCK_TOKENS = 128


floor_score = -1e30


def shifted(value, axis, steps):
    count = lax.axis_size(axis)
    pairs = [(source, (source + steps) % count) for source in range(count)]
    return lax.ppermute(value, axis, pairs)


def joined(value, axis, combine):
    everything = jax.tree.map(lambda part: lax.all_gather(part, axis), value)
    first = jax.tree.map(lambda part: part[0], everything)

    def lap(k, so_far):
        return combine(so_far, jax.tree.map(lambda part: part[k], everything))

    return lax.fori_loop(1, lax.axis_size(axis), lap, first)


def fold_scores(running, scores, value_row_block, allowed):
    highest, totals, accumulated = running
    masked = jnp.where(allowed, scores, floor_score)
    new_highest = jnp.maximum(highest, jnp.max(masked, axis=-1))
    weights = jnp.where(allowed, jnp.exp(scores - new_highest[:, None]), 0.0)
    fading = jnp.exp(highest - new_highest)
    totals = totals * fading + jnp.sum(weights, axis=-1)
    accumulated = accumulated * fading[:, None] + jnp.dot(
        weights.astype(jnp.bfloat16), value_row_block, preferred_element_type=jnp.float32
    )
    return (new_highest, totals, accumulated)


def combine(first_part, second_part):
    first_high, first_total, first_acc = first_part
    second_high, second_total, second_acc = second_part
    highest = jnp.maximum(first_high, second_high)
    first_fade = jnp.exp(first_high - highest)
    second_fade = jnp.exp(second_high - highest)
    totals = first_total * first_fade + second_total * second_fade
    accumulated = first_acc * first_fade[..., None] + second_acc * second_fade[..., None]
    return (highest, totals, accumulated)


def per_device(
    self_query_columns, text_key_value, cross_query_columns, image_kv, block_images, image_owner
):
    row_count = self_query_columns.shape[0]
    heads_here = self_query_columns.shape[1] // HEAD_SIZE
    block_count = row_count // MASK_BLOCK_TOKENS
    position = lax.axis_index("blk")
    cycle_size = lax.axis_size("blk")
    score_scale = 1.0 / math.sqrt(HEAD_SIZE)
    self_queries = self_query_columns.reshape(row_count * heads_here, HEAD_SIZE)
    query_pos = (
        position * row_count + jnp.arange(row_count * heads_here, dtype=jnp.int32) // heads_here
    )
    gathered = lax.all_gather(cross_query_columns, "enc", axis=1, tiled=True)
    query_group_width = gathered.shape[1] // HEAD_SIZE
    cross_queries = gathered.reshape(block_count, MASK_BLOCK_TOKENS * query_group_width, HEAD_SIZE)
    slot_ids = jnp.arange(cycle_size, dtype=jnp.int32)
    placed = (image_owner[:, None] == slot_ids[None, :]).astype(jnp.int32)
    seen_slots = jnp.sum(block_images[:, :, None] * placed[None, :, :], axis=1)

    def self_update(states, text_piece, source):
        key_row_block = text_piece[:, 0, :]
        value_row_block = text_piece[:, 1, :]

        def self_attend(running):
            scores = (
                jnp.einsum(
                    "qd,kd->qk", self_queries, key_row_block, preferred_element_type=jnp.float32
                )
                * score_scale
            )
            key_pos = source * row_count + jnp.arange(key_row_block.shape[0], dtype=jnp.int32)
            allowed = key_pos[None, :] <= query_pos[:, None]
            return fold_scores(running, scores, value_row_block, allowed)

        return lax.cond(source <= position, self_attend, lambda running: running, states)

    def cross_update(states, image_tile, flags):
        key_row_block = image_tile[0]
        value_row_block = image_tile[1]

        def per_block(carried, element):
            queries, highest, totals, accumulated, seen_flag = element

            def per_attend(running):
                scores = (
                    jnp.einsum(
                        "qd,kd->qk", queries, key_row_block, preferred_element_type=jnp.float32
                    )
                    * score_scale
                )
                return fold_scores(running, scores, value_row_block, True)

            updated = lax.cond(
                seen_flag > 0, per_attend, lambda running: running, (highest, totals, accumulated)
            )
            return (carried, updated)

        _, updated = lax.scan(per_block, 0, (cross_queries, states[0], states[1], states[2], flags))
        return updated

    def absorb(states, text_piece, image_tile, source):
        self_states = self_update(states[0], text_piece, source)
        cross_states = cross_update(
            states[1], image_tile, lax.dynamic_index_in_dim(seen_slots, source, 1, keepdims=False)
        )
        return (self_states, cross_states)

    self_rows = row_count * heads_here
    cross_rows = MASK_BLOCK_TOKENS * query_group_width
    self_init = (
        jnp.full((self_rows,), floor_score, jnp.float32),
        jnp.zeros((self_rows,), jnp.float32),
        jnp.zeros((self_rows, HEAD_SIZE), jnp.float32),
    )
    cross_init = (
        jnp.full((block_count, cross_rows), floor_score, jnp.float32),
        jnp.zeros((block_count, cross_rows), jnp.float32),
        jnp.zeros((block_count, cross_rows, HEAD_SIZE), jnp.float32),
    )

    def advance(step_index, carried):
        text_piece, image_piece, states = carried
        source = (position - step_index) % cycle_size
        states = absorb(states, text_piece, image_piece[0], source)
        moved = shifted((text_piece, image_piece), "blk", 1)
        text_piece, image_piece = moved
        return (text_piece, image_piece, states)

    text_piece, image_piece, states = lax.fori_loop(
        0, cycle_size - 1, advance, (text_key_value, image_kv, (self_init, cross_init))
    )
    states = absorb(states, text_piece, image_piece[0], (position + 1) % cycle_size)
    self_state, cross_state = states
    self_out = (
        (self_state[2] / self_state[1][:, None])
        .reshape(row_count, heads_here * HEAD_SIZE)
        .astype(jnp.bfloat16)
    )
    highest = cross_state[0].reshape(row_count, query_group_width)
    totals = cross_state[1].reshape(row_count, query_group_width)
    accumulated = cross_state[2].reshape(row_count, query_group_width, HEAD_SIZE)
    highest, totals, accumulated = joined((highest, totals, accumulated), "enc", combine)
    first_head = lax.axis_index("enc") * heads_here
    own_totals = lax.dynamic_slice_in_dim(totals, first_head, heads_here, 1)
    own_acc = lax.dynamic_slice_in_dim(accumulated, first_head, heads_here, 1)
    cross_out = (
        (own_acc / own_totals[..., None])
        .reshape(row_count, heads_here * HEAD_SIZE)
        .astype(jnp.bfloat16)
    )
    return (self_out, cross_out)


def solution(mesh):
    placed = (
        P("blk", ("tp", "enc")),
        P("blk", None, "tp"),
        P("blk", ("tp", "enc")),
        P("blk", None, "enc", "tp"),
        P("blk", None),
        P(),
    )
    return jax.shard_map(
        per_device,
        mesh=mesh,
        in_specs=placed,
        out_specs=(P("blk", ("tp", "enc")), P("blk", ("tp", "enc"))),
        check_vma=False,
    )
```

profile of v0, /device:TPU:16, one launch (start us, length us, event | category | flops | bytes accessed | tf_op | source)
XLA Modules:
  0.0 745.3 jit_solution(14513671628548066431)
XLA Ops:
  13.6 27.4 %all-gather.3.cloned.1.call-done = bf16[512,1024]{1,0:T(8,128)(2,1)} async-done(((bf16[512,256]{1,0:T(8,128)(2,1)}), bf16[512,1024]{1,0:T(8,128)(2,1)}) %all-gather.3.cloned.1.call-update) | async-done | bytes 1048592 | tf_op jit(solution)/shard_map/all_gather | solution.py:68
  44.3 540.4 %while.102 = (s32[]{:T(128)}, bf16[512,2,128]{2,0,1:T(8,128)(2,1)}, bf16[1,2,1601,128]{3,1,2,0:T(2,128)(2,1)}, f32[1024]{0:T(1024)S(1)}, f32[1024]{0:T(1024)S(1)...) while((s32[]{:T(128)}, bf16[512,2,128]{2,0,1:T(8,128)(2,1)}, ...), condition=%wide.region_12.13_spmd.clone, body=%wide.region_1.12_spmd.clone.sunk | while | flops 1128814080 | bytes 45952056 | solution.py:144
  54.3 13.9 %while.103 = (s32[]{:T(128)}, f32[4,1024]{1,0:T(4,128)S(1)}, f32[4,1024]{1,0:T(4,128)S(1)}, f32[4,1024,128]{2,1,0:T(8,128)S(1)}, s32[4]{0:T(128)S(1)}, /*index=5...) while((s32[]{:T(128)}, f32[4,1024]{1,0:T(4,128)S(1)}, ...), condition=%wide.region_11.11_spmd.clone, body=%wide.region_6.10_spmd.clone.sunk | while | flops 852764672 | bytes 23999756 | solution.py:113
  68.2 4.7 conditional.11
  79.0 17.0 %collective-permute-start.1 = (bf16[1,2,1601,128]{3,1,2,0:T(2,128)(2,1)}, bf16[1,2,1601,128]{3,1,2,0:T(2,128)(2,1)}, u32[]{:S(2)}, u32[]{:S(2)}) collective-permute-start(bf16[1,2,1601,128]{3,1,2,0:T(2,128)(2,1)} %copy.117), channel_id=1, source_target_pairs={{0,16},{16,32},{32,48},{48,64},{64,80},{80,96},{96,112},{112,128},... | collective-permute-start | bytes 2459144 | tf_op jit(solution)/shard_map/while/body/eval_jaxpr/ppermute | solution.py:18
  97.4 13.9 %while.103 = (s32[]{:T(128)}, f32[4,1024]{1,0:T(4,128)S(1)}, f32[4,1024]{1,0:T(4,128)S(1)}, f32[4,1024,128]{2,1,0:T(8,128)S(1)}, s32[4]{0:T(128)S(1)}, /*index=5...) while((s32[]{:T(128)}, f32[4,1024]{1,0:T(4,128)S(1)}, ...), condition=%wide.region_11.11_spmd.clone, body=%wide.region_6.10_spmd.clone.sunk | while | flops 852764672 | bytes 23999756 | solution.py:113
  111.3 4.7 conditional.11
  125.1 13.9 %while.103 = (s32[]{:T(128)}, f32[4,1024]{1,0:T(4,128)S(1)}, f32[4,1024]{1,0:T(4,128)S(1)}, f32[4,1024,128]{2,1,0:T(8,128)S(1)}, s32[4]{0:T(128)S(1)}, /*index=5...) while((s32[]{:T(128)}, f32[4,1024]{1,0:T(4,128)S(1)}, ...), condition=%wide.region_11.11_spmd.clone, body=%wide.region_6.10_spmd.clone.sunk | while | flops 852764672 | bytes 23999756 | solution.py:113
  139.1 11.8 %collective-permute-done.1 = bf16[1,2,1601,128]{3,1,2,0:T(2,128)(2,1)} collective-permute-done((bf16[1,2,1601,128]{3,1,2,0:T(2,128)(2,1)}, bf16[1,2,1601,128]{3,1,2,0:T(2,128)(2,1)}, u32[]{:S(2)}, u32[]{:S(2)}) %collective-permute-start.1) | collective-permute-done | bytes 819744 | tf_op jit(solution)/shard_map/while/body/eval_jaxpr/ppermute | solution.py:18
  152.5 11.2 %collective-permute-start = (bf16[512,2,128]{2,0,1:T(8,128)(2,1)}, bf16[512,2,128]{2,0,1:T(8,128)(2,1)}, u32[]{:S(2)}, u32[]{:S(2)}) collective-permute-start(bf16[512,2,128]{2,0,1:T(8,128)(2,1)} %copy.116), channel_id=1, source_target_pairs={{0,16},{16,32},{32,48},{48,64},{64,80},{80,96},{96,112},{112,128},... | collective-permute-start | bytes 786440 | tf_op jit(solution)/shard_map/while/body/eval_jaxpr/ppermute | solution.py:18
  167.4 13.9 %while.103 = (s32[]{:T(128)}, f32[4,1024]{1,0:T(4,128)S(1)}, f32[4,1024]{1,0:T(4,128)S(1)}, f32[4,1024,128]{2,1,0:T(8,128)S(1)}, s32[4]{0:T(128)S(1)}, /*index=5...) while((s32[]{:T(128)}, f32[4,1024]{1,0:T(4,128)S(1)}, ...), condition=%wide.region_11.11_spmd.clone, body=%wide.region_6.10_spmd.clone.sunk | while | flops 852764672 | bytes 23999756 | solution.py:113
  181.3 3.7 collective-permute-done.1
  186.7 4.5 collective-permute-start
  195.4 13.9 %while.103 = (s32[]{:T(128)}, f32[4,1024]{1,0:T(4,128)S(1)}, f32[4,1024]{1,0:T(4,128)S(1)}, f32[4,1024,128]{2,1,0:T(8,128)S(1)}, s32[4]{0:T(128)S(1)}, /*index=5...) while((s32[]{:T(128)}, f32[4,1024]{1,0:T(4,128)S(1)}, ...), condition=%wide.region_11.11_spmd.clone, body=%wide.region_6.10_spmd.clone.sunk | while | flops 852764672 | bytes 23999756 | solution.py:113
  214.1 3.6 collective-permute-start
  220.1 49.1 %collective-permute-start.1 = (bf16[1,2,1601,128]{3,1,2,0:T(2,128)(2,1)}, bf16[1,2,1601,128]{3,1,2,0:T(2,128)(2,1)}, u32[]{:S(2)}, u32[]{:S(2)}) collective-permute-start(bf16[1,2,1601,128]{3,1,2,0:T(2,128)(2,1)} %copy.117), channel_id=1, source_target_pairs={{0,16},{16,32},{32,48},{48,64},{64,80},{80,96},{96,112},{112,128},... | collective-permute-start | bytes 2459144 | tf_op jit(solution)/shard_map/while/body/eval_jaxpr/ppermute | solution.py:18
  270.6 35.7 %while.103 = (s32[]{:T(128)}, f32[4,1024]{1,0:T(4,128)S(1)}, f32[4,1024]{1,0:T(4,128)S(1)}, f32[4,1024,128]{2,1,0:T(8,128)S(1)}, s32[4]{0:T(128)S(1)}, /*index=5...) while((s32[]{:T(128)}, f32[4,1024]{1,0:T(4,128)S(1)}, ...), condition=%wide.region_11.11_spmd.clone, body=%wide.region_6.10_spmd.clone.sunk | while | flops 852764672 | bytes 23999756 | solution.py:113
  273.1 7.3 conditional.12
  283.9 7.3 conditional.12
  294.6 7.3 conditional.12
  311.8 28.5 %while.103 = (s32[]{:T(128)}, f32[4,1024]{1,0:T(4,128)S(1)}, f32[4,1024]{1,0:T(4,128)S(1)}, f32[4,1024,128]{2,1,0:T(8,128)S(1)}, s32[4]{0:T(128)S(1)}, /*index=5...) while((s32[]{:T(128)}, f32[4,1024]{1,0:T(4,128)S(1)}, ...), condition=%wide.region_11.11_spmd.clone, body=%wide.region_6.10_spmd.clone.sunk | while | flops 852764672 | bytes 23999756 | solution.py:113
  314.4 7.3 conditional.12
  325.1 7.3 conditional.12
  342.1 9.9 %collective-permute-start = (bf16[512,2,128]{2,0,1:T(8,128)(2,1)}, bf16[512,2,128]{2,0,1:T(8,128)(2,1)}, u32[]{:S(2)}, u32[]{:S(2)}) collective-permute-start(bf16[512,2,128]{2,0,1:T(8,128)(2,1)} %copy.116), channel_id=1, source_target_pairs={{0,16},{16,32},{32,48},{48,64},{64,80},{80,96},{96,112},{112,128},... | collective-permute-start | bytes 786440 | tf_op jit(solution)/shard_map/while/body/eval_jaxpr/ppermute | solution.py:18
  355.6 13.9 %while.103 = (s32[]{:T(128)}, f32[4,1024]{1,0:T(4,128)S(1)}, f32[4,1024]{1,0:T(4,128)S(1)}, f32[4,1024,128]{2,1,0:T(8,128)S(1)}, s32[4]{0:T(128)S(1)}, /*index=5...) while((s32[]{:T(128)}, f32[4,1024]{1,0:T(4,128)S(1)}, ...), condition=%wide.region_11.11_spmd.clone, body=%wide.region_6.10_spmd.clone.sunk | while | flops 852764672 | bytes 23999756 | solution.py:113
  372.9 4.5 collective-permute-start
  381.1 13.9 %while.103 = (s32[]{:T(128)}, f32[4,1024]{1,0:T(4,128)S(1)}, f32[4,1024]{1,0:T(4,128)S(1)}, f32[4,1024,128]{2,1,0:T(8,128)S(1)}, s32[4]{0:T(128)S(1)}, /*index=5...) while((s32[]{:T(128)}, f32[4,1024]{1,0:T(4,128)S(1)}, ...), condition=%wide.region_11.11_spmd.clone, body=%wide.region_6.10_spmd.clone.sunk | while | flops 852764672 | bytes 23999756 | solution.py:113
  405.7 21.2 %while.103 = (s32[]{:T(128)}, f32[4,1024]{1,0:T(4,128)S(1)}, f32[4,1024]{1,0:T(4,128)S(1)}, f32[4,1024,128]{2,1,0:T(8,128)S(1)}, s32[4]{0:T(128)S(1)}, /*index=5...) while((s32[]{:T(128)}, f32[4,1024]{1,0:T(4,128)S(1)}, ...), condition=%wide.region_11.11_spmd.clone, body=%wide.region_6.10_spmd.clone.sunk | while | flops 852764672 | bytes 23999756 | solution.py:113
  418.6 7.3 conditional.12
  432.3 13.9 %while.103 = (s32[]{:T(128)}, f32[4,1024]{1,0:T(4,128)S(1)}, f32[4,1024]{1,0:T(4,128)S(1)}, f32[4,1024,128]{2,1,0:T(8,128)S(1)}, s32[4]{0:T(128)S(1)}, /*index=5...) while((s32[]{:T(128)}, f32[4,1024]{1,0:T(4,128)S(1)}, ...), condition=%wide.region_11.11_spmd.clone, body=%wide.region_6.10_spmd.clone.sunk | while | flops 852764672 | bytes 23999756 | solution.py:113
  446.3 5.5 collective-permute-done.1
  453.5 21.8 %collective-permute-start = (bf16[512,2,128]{2,0,1:T(8,128)(2,1)}, bf16[512,2,128]{2,0,1:T(8,128)(2,1)}, u32[]{:S(2)}, u32[]{:S(2)}) collective-permute-start(bf16[512,2,128]{2,0,1:T(8,128)(2,1)} %copy.116), channel_id=1, source_target_pairs={{0,16},{16,32},{32,48},{48,64},{64,80},{80,96},{96,112},{112,128},... | collective-permute-start | bytes 786440 | tf_op jit(solution)/shard_map/while/body/eval_jaxpr/ppermute | solution.py:18
  479.0 13.9 %while.103 = (s32[]{:T(128)}, f32[4,1024]{1,0:T(4,128)S(1)}, f32[4,1024]{1,0:T(4,128)S(1)}, f32[4,1024,128]{2,1,0:T(8,128)S(1)}, s32[4]{0:T(128)S(1)}, /*index=5...) while((s32[]{:T(128)}, f32[4,1024]{1,0:T(4,128)S(1)}, ...), condition=%wide.region_11.11_spmd.clone, body=%wide.region_6.10_spmd.clone.sunk | while | flops 852764672 | bytes 23999756 | solution.py:113
  495.2 4.2 collective-permute-start
  503.1 13.9 %while.103 = (s32[]{:T(128)}, f32[4,1024]{1,0:T(4,128)S(1)}, f32[4,1024]{1,0:T(4,128)S(1)}, f32[4,1024,128]{2,1,0:T(8,128)S(1)}, s32[4]{0:T(128)S(1)}, /*index=5...) while((s32[]{:T(128)}, f32[4,1024]{1,0:T(4,128)S(1)}, ...), condition=%wide.region_11.11_spmd.clone, body=%wide.region_6.10_spmd.clone.sunk | while | flops 852764672 | bytes 23999756 | solution.py:113
  526.5 13.9 %while.103 = (s32[]{:T(128)}, f32[4,1024]{1,0:T(4,128)S(1)}, f32[4,1024]{1,0:T(4,128)S(1)}, f32[4,1024,128]{2,1,0:T(8,128)S(1)}, s32[4]{0:T(128)S(1)}, /*index=5...) while((s32[]{:T(128)}, f32[4,1024]{1,0:T(4,128)S(1)}, ...), condition=%wide.region_11.11_spmd.clone, body=%wide.region_6.10_spmd.clone.sunk | while | flops 852764672 | bytes 23999756 | solution.py:113
  540.4 6.7 collective-permute-done
  547.1 12.0 %collective-permute-done.1 = bf16[1,2,1601,128]{3,1,2,0:T(2,128)(2,1)} collective-permute-done((bf16[1,2,1601,128]{3,1,2,0:T(2,128)(2,1)}, bf16[1,2,1601,128]{3,1,2,0:T(2,128)(2,1)}, u32[]{:S(2)}, u32[]{:S(2)}) %collective-permute-start.1) | collective-permute-done | bytes 819744 | tf_op jit(solution)/shard_map/while/body/eval_jaxpr/ppermute | solution.py:18
  564.5 13.9 %while.103 = (s32[]{:T(128)}, f32[4,1024]{1,0:T(4,128)S(1)}, f32[4,1024]{1,0:T(4,128)S(1)}, f32[4,1024,128]{2,1,0:T(8,128)S(1)}, s32[4]{0:T(128)S(1)}, /*index=5...) while((s32[]{:T(128)}, f32[4,1024]{1,0:T(4,128)S(1)}, ...), condition=%wide.region_11.11_spmd.clone, body=%wide.region_6.10_spmd.clone.sunk | while | flops 852764672 | bytes 23999756 | solution.py:113
  578.4 6.3 collective-permute-done.1
  587.5 17.1 %while.99 = (s32[]{:T(128)}, f32[4,1024]{1,0:T(4,128)S(1)}, f32[4,1024]{1,0:T(4,128)S(1)}, f32[4,1024,128]{2,1,0:T(8,128)}, s32[4]{0:T(128)S(1)}, /*index=5*/f32...) while((s32[]{:T(128)}, f32[4,1024]{1,0:T(4,128)S(1)}, ...), condition=%wide.region_22.23_spmd, body=%wide.region_17.22_spmd.sunk | while | flops 852764672 | bytes 24000288 | solution.py:113
  607.3 12.1 %all_gather.13 = f32[4,512,8]{1,2,0:T(8,128)S(1)} all-gather(f32[1,512,8]{1,2,0:T(8,128)S(1)} %copy.58), channel_id=1, replica_groups=mesh['blk'=16,'tp'=4,'enc'=4] {'enc'}, dimensions={0}, use_global_device_ids=true | all-gather | bytes 81920 | tf_op jit(solution)/shard_map/all_gather | solution.py:22
  619.5 11.9 %all_gather.14 = f32[4,512,8]{1,2,0:T(8,128)S(1)} all-gather(f32[1,512,8]{1,2,0:T(8,128)S(1)} %copy.59), channel_id=1, replica_groups=mesh['blk'=16,'tp'=4,'enc'=4] {'enc'}, dimensions={0}, use_global_device_ids=true | all-gather | bytes 81920 | tf_op jit(solution)/shard_map/all_gather | solution.py:22
  631.3 91.3 %all-gather.5.cloned.1.call-done = f32[4,512,8,128]{3,2,1,0:T(8,128)} async-done(((f32[1,512,8,128]{3,2,1,0:T(8,128)}), f32[4,512,8,128]{3,2,1,0:T(8,128)}) %all-gather.5.cloned.1.call-update) | async-done | bytes 8388624 | tf_op jit(solution)/shard_map/all_gather | solution.py:22
  724.4 12.4 %while.100 = (s32[]{:T(128)}, f32[512,8]{0,1:T(8,128)S(1)}, f32[512,8]{0,1:T(8,128)S(1)}, f32[512,8,128]{2,1,0:T(8,128)S(1)}, f32[4,512,8]{1,2,0:T(8,128)S(1)}, ...) while((s32[]{:T(128)}, f32[512,8]{0,1:T(8,128)S(1)}, ...), condition=%wide.region_24.25_spmd, body=%wide.region_23.24_spmd.sunk | while | flops 1597445 | bytes 6520975 | solution.py:28
  724.7 3.8 fusion.85
  728.8 3.8 fusion.85
  732.9 3.8 fusion.85
  (797 shorter events, 360.4 us)
Async XLA Ops:
  7.2 4.9 copy-start.3
  7.2 5.7 copy-start.4
  7.2 33.8 %all-gather.3.cloned.1.call-start = ((), (), s32[]{:S(2)}) async-start(), calls=%async_computation | async-start | bytes 1310720 | tf_op jit(solution)/shard_map/all_gather | solution.py:68
  9.7 712.9 %all-gather.5.cloned.1.call-start = ((), (), s32[]{:S(2)}) async-start(), calls=%async_computation.1 | async-start | bytes 10485760 | tf_op jit(solution)/shard_map/all_gather | solution.py:22
  46.0 26.9 %collective-permute-start = (bf16[512,2,128]{2,0,1:T(8,128)(2,1)}, bf16[512,2,128]{2,0,1:T(8,128)(2,1)}, u32[]{:S(2)}, u32[]{:S(2)}) collective-permute-start(bf16[512,2,128]{2,0,1:T(8,128)(2,1)} %copy.116), channel_id=1, source_target_pairs={{0,16},{16,32},{32,48},{48,64},{64,80},{80,96},{96,112},{112,128},... | collective-permute-start | bytes 786440 | tf_op jit(solution)/shard_map/while/body/eval_jaxpr/ppermute | solution.py:18
  49.9 23.1 %collective-permute-start.1 = (bf16[1,2,1601,128]{3,1,2,0:T(2,128)(2,1)}, bf16[1,2,1601,128]{3,1,2,0:T(2,128)(2,1)}, u32[]{:S(2)}, u32[]{:S(2)}) collective-permute-start(bf16[1,2,1601,128]{3,1,2,0:T(2,128)(2,1)} %copy.117), channel_id=1, source_target_pairs={{0,16},{16,32},{32,48},{48,64},{64,80},{80,96},{96,112},{112,128},... | collective-permute-start | bytes 2459144 | tf_op jit(solution)/shard_map/while/body/eval_jaxpr/ppermute | solution.py:18
  68.2 2.1 copy-start
  72.1 0.8 copy-start.1
  74.6 41.5 %collective-permute-start = (bf16[512,2,128]{2,0,1:T(8,128)(2,1)}, bf16[512,2,128]{2,0,1:T(8,128)(2,1)}, u32[]{:S(2)}, u32[]{:S(2)}) collective-permute-start(bf16[512,2,128]{2,0,1:T(8,128)(2,1)} %copy.116), channel_id=1, source_target_pairs={{0,16},{16,32},{32,48},{48,64},{64,80},{80,96},{96,112},{112,128},... | collective-permute-start | bytes 786440 | tf_op jit(solution)/shard_map/while/body/eval_jaxpr/ppermute | solution.py:18
  79.0 37.1 %collective-permute-start.1 = (bf16[1,2,1601,128]{3,1,2,0:T(2,128)(2,1)}, bf16[1,2,1601,128]{3,1,2,0:T(2,128)(2,1)}, u32[]{:S(2)}, u32[]{:S(2)}) collective-permute-start(bf16[1,2,1601,128]{3,1,2,0:T(2,128)(2,1)} %copy.117), channel_id=1, source_target_pairs={{0,16},{16,32},{32,48},{48,64},{64,80},{80,96},{96,112},{112,128},... | collective-permute-start | bytes 2459144 | tf_op jit(solution)/shard_map/while/body/eval_jaxpr/ppermute | solution.py:18
  111.4 2.1 copy-start
  115.3 0.8 copy-start.1
  117.8 21.3 %collective-permute-start = (bf16[512,2,128]{2,0,1:T(8,128)(2,1)}, bf16[512,2,128]{2,0,1:T(8,128)(2,1)}, u32[]{:S(2)}, u32[]{:S(2)}) collective-permute-start(bf16[512,2,128]{2,0,1:T(8,128)(2,1)} %copy.116), channel_id=1, source_target_pairs={{0,16},{16,32},{32,48},{48,64},{64,80},{80,96},{96,112},{112,128},... | collective-permute-start | bytes 786440 | tf_op jit(solution)/shard_map/while/body/eval_jaxpr/ppermute | solution.py:18
  121.1 29.7 %collective-permute-start.1 = (bf16[1,2,1601,128]{3,1,2,0:T(2,128)(2,1)}, bf16[1,2,1601,128]{3,1,2,0:T(2,128)(2,1)}, u32[]{:S(2)}, u32[]{:S(2)}) collective-permute-start(bf16[1,2,1601,128]{3,1,2,0:T(2,128)(2,1)} %copy.117), channel_id=1, source_target_pairs={{0,16},{16,32},{32,48},{48,64},{64,80},{80,96},{96,112},{112,128},... | collective-permute-start | bytes 2459144 | tf_op jit(solution)/shard_map/while/body/eval_jaxpr/ppermute | solution.py:18
  152.5 28.8 %collective-permute-start = (bf16[512,2,128]{2,0,1:T(8,128)(2,1)}, bf16[512,2,128]{2,0,1:T(8,128)(2,1)}, u32[]{:S(2)}, u32[]{:S(2)}) collective-permute-start(bf16[512,2,128]{2,0,1:T(8,128)(2,1)} %copy.116), channel_id=1, source_target_pairs={{0,16},{16,32},{32,48},{48,64},{64,80},{80,96},{96,112},{112,128},... | collective-permute-start | bytes 786440 | tf_op jit(solution)/shard_map/while/body/eval_jaxpr/ppermute | solution.py:18
  166.0 19.0 %collective-permute-start.1 = (bf16[1,2,1601,128]{3,1,2,0:T(2,128)(2,1)}, bf16[1,2,1601,128]{3,1,2,0:T(2,128)(2,1)}, u32[]{:S(2)}, u32[]{:S(2)}) collective-permute-start(bf16[1,2,1601,128]{3,1,2,0:T(2,128)(2,1)} %copy.117), channel_id=1, source_target_pairs={{0,16},{16,32},{32,48},{48,64},{64,80},{80,96},{96,112},{112,128},... | collective-permute-start | bytes 2459144 | tf_op jit(solution)/shard_map/while/body/eval_jaxpr/ppermute | solution.py:18
  186.7 22.7 %collective-permute-start = (bf16[512,2,128]{2,0,1:T(8,128)(2,1)}, bf16[512,2,128]{2,0,1:T(8,128)(2,1)}, u32[]{:S(2)}, u32[]{:S(2)}) collective-permute-start(bf16[512,2,128]{2,0,1:T(8,128)(2,1)} %copy.116), channel_id=1, source_target_pairs={{0,16},{16,32},{32,48},{48,64},{64,80},{80,96},{96,112},{112,128},... | collective-permute-start | bytes 786440 | tf_op jit(solution)/shard_map/while/body/eval_jaxpr/ppermute | solution.py:18
  193.5 19.0 %collective-permute-start.1 = (bf16[1,2,1601,128]{3,1,2,0:T(2,128)(2,1)}, bf16[1,2,1601,128]{3,1,2,0:T(2,128)(2,1)}, u32[]{:S(2)}, u32[]{:S(2)}) collective-permute-start(bf16[1,2,1601,128]{3,1,2,0:T(2,128)(2,1)} %copy.117), channel_id=1, source_target_pairs={{0,16},{16,32},{32,48},{48,64},{64,80},{80,96},{96,112},{112,128},... | collective-permute-start | bytes 2459144 | tf_op jit(solution)/shard_map/while/body/eval_jaxpr/ppermute | solution.py:18
  214.1 92.3 %collective-permute-start = (bf16[512,2,128]{2,0,1:T(8,128)(2,1)}, bf16[512,2,128]{2,0,1:T(8,128)(2,1)}, u32[]{:S(2)}, u32[]{:S(2)}) collective-permute-start(bf16[512,2,128]{2,0,1:T(8,128)(2,1)} %copy.116), channel_id=1, source_target_pairs={{0,16},{16,32},{32,48},{48,64},{64,80},{80,96},{96,112},{112,128},... | collective-permute-start | bytes 786440 | tf_op jit(solution)/shard_map/while/body/eval_jaxpr/ppermute | solution.py:18
  220.1 86.3 %collective-permute-start.1 = (bf16[1,2,1601,128]{3,1,2,0:T(2,128)(2,1)}, bf16[1,2,1601,128]{3,1,2,0:T(2,128)(2,1)}, u32[]{:S(2)}, u32[]{:S(2)}) collective-permute-start(bf16[1,2,1601,128]{3,1,2,0:T(2,128)(2,1)} %copy.117), channel_id=1, source_target_pairs={{0,16},{16,32},{32,48},{48,64},{64,80},{80,96},{96,112},{112,128},... | collective-permute-start | bytes 2459144 | tf_op jit(solution)/shard_map/while/body/eval_jaxpr/ppermute | solution.py:18
  308.1 32.3 %collective-permute-start = (bf16[512,2,128]{2,0,1:T(8,128)(2,1)}, bf16[512,2,128]{2,0,1:T(8,128)(2,1)}, u32[]{:S(2)}, u32[]{:S(2)}) collective-permute-start(bf16[512,2,128]{2,0,1:T(8,128)(2,1)} %copy.116), channel_id=1, source_target_pairs={{0,16},{16,32},{32,48},{48,64},{64,80},{80,96},{96,112},{112,128},... | collective-permute-start | bytes 786440 | tf_op jit(solution)/shard_map/while/body/eval_jaxpr/ppermute | solution.py:18
  310.4 29.9 %collective-permute-start.1 = (bf16[1,2,1601,128]{3,1,2,0:T(2,128)(2,1)}, bf16[1,2,1601,128]{3,1,2,0:T(2,128)(2,1)}, u32[]{:S(2)}, u32[]{:S(2)}) collective-permute-start(bf16[1,2,1601,128]{3,1,2,0:T(2,128)(2,1)} %copy.117), channel_id=1, source_target_pairs={{0,16},{16,32},{32,48},{48,64},{64,80},{80,96},{96,112},{112,128},... | collective-permute-start | bytes 2459144 | tf_op jit(solution)/shard_map/while/body/eval_jaxpr/ppermute | solution.py:18
  342.1 27.5 %collective-permute-start = (bf16[512,2,128]{2,0,1:T(8,128)(2,1)}, bf16[512,2,128]{2,0,1:T(8,128)(2,1)}, u32[]{:S(2)}, u32[]{:S(2)}) collective-permute-start(bf16[512,2,128]{2,0,1:T(8,128)(2,1)} %copy.116), channel_id=1, source_target_pairs={{0,16},{16,32},{32,48},{48,64},{64,80},{80,96},{96,112},{112,128},... | collective-permute-start | bytes 786440 | tf_op jit(solution)/shard_map/while/body/eval_jaxpr/ppermute | solution.py:18
  354.3 17.0 %collective-permute-start.1 = (bf16[1,2,1601,128]{3,1,2,0:T(2,128)(2,1)}, bf16[1,2,1601,128]{3,1,2,0:T(2,128)(2,1)}, u32[]{:S(2)}, u32[]{:S(2)}) collective-permute-start(bf16[1,2,1601,128]{3,1,2,0:T(2,128)(2,1)} %copy.117), channel_id=1, source_target_pairs={{0,16},{16,32},{32,48},{48,64},{64,80},{80,96},{96,112},{112,128},... | collective-permute-start | bytes 2459144 | tf_op jit(solution)/shard_map/while/body/eval_jaxpr/ppermute | solution.py:18
  372.9 22.1 %collective-permute-start = (bf16[512,2,128]{2,0,1:T(8,128)(2,1)}, bf16[512,2,128]{2,0,1:T(8,128)(2,1)}, u32[]{:S(2)}, u32[]{:S(2)}) collective-permute-start(bf16[512,2,128]{2,0,1:T(8,128)(2,1)} %copy.116), channel_id=1, source_target_pairs={{0,16},{16,32},{32,48},{48,64},{64,80},{80,96},{96,112},{112,128},... | collective-permute-start | bytes 786440 | tf_op jit(solution)/shard_map/while/body/eval_jaxpr/ppermute | solution.py:18
  379.7 18.9 %collective-permute-start.1 = (bf16[1,2,1601,128]{3,1,2,0:T(2,128)(2,1)}, bf16[1,2,1601,128]{3,1,2,0:T(2,128)(2,1)}, u32[]{:S(2)}, u32[]{:S(2)}) collective-permute-start(bf16[1,2,1601,128]{3,1,2,0:T(2,128)(2,1)} %copy.117), channel_id=1, source_target_pairs={{0,16},{16,32},{32,48},{48,64},{64,80},{80,96},{96,112},{112,128},... | collective-permute-start | bytes 2459144 | tf_op jit(solution)/shard_map/while/body/eval_jaxpr/ppermute | solution.py:18
  400.3 26.6 %collective-permute-start = (bf16[512,2,128]{2,0,1:T(8,128)(2,1)}, bf16[512,2,128]{2,0,1:T(8,128)(2,1)}, u32[]{:S(2)}, u32[]{:S(2)}) collective-permute-start(bf16[512,2,128]{2,0,1:T(8,128)(2,1)} %copy.116), channel_id=1, source_target_pairs={{0,16},{16,32},{32,48},{48,64},{64,80},{80,96},{96,112},{112,128},... | collective-permute-start | bytes 786440 | tf_op jit(solution)/shard_map/while/body/eval_jaxpr/ppermute | solution.py:18
  404.3 22.6 %collective-permute-start.1 = (bf16[1,2,1601,128]{3,1,2,0:T(2,128)(2,1)}, bf16[1,2,1601,128]{3,1,2,0:T(2,128)(2,1)}, u32[]{:S(2)}, u32[]{:S(2)}) collective-permute-start(bf16[1,2,1601,128]{3,1,2,0:T(2,128)(2,1)} %copy.117), channel_id=1, source_target_pairs={{0,16},{16,32},{32,48},{48,64},{64,80},{80,96},{96,112},{112,128},... | collective-permute-start | bytes 2459144 | tf_op jit(solution)/shard_map/while/body/eval_jaxpr/ppermute | solution.py:18
  428.6 17.7 %collective-permute-start = (bf16[512,2,128]{2,0,1:T(8,128)(2,1)}, bf16[512,2,128]{2,0,1:T(8,128)(2,1)}, u32[]{:S(2)}, u32[]{:S(2)}) collective-permute-start(bf16[512,2,128]{2,0,1:T(8,128)(2,1)} %copy.116), channel_id=1, source_target_pairs={{0,16},{16,32},{32,48},{48,64},{64,80},{80,96},{96,112},{112,128},... | collective-permute-start | bytes 786440 | tf_op jit(solution)/shard_map/while/body/eval_jaxpr/ppermute | solution.py:18
  431.0 20.9 %collective-permute-start.1 = (bf16[1,2,1601,128]{3,1,2,0:T(2,128)(2,1)}, bf16[1,2,1601,128]{3,1,2,0:T(2,128)(2,1)}, u32[]{:S(2)}, u32[]{:S(2)}) collective-permute-start(bf16[1,2,1601,128]{3,1,2,0:T(2,128)(2,1)} %copy.117), channel_id=1, source_target_pairs={{0,16},{16,32},{32,48},{48,64},{64,80},{80,96},{96,112},{112,128},... | collective-permute-start | bytes 2459144 | tf_op jit(solution)/shard_map/while/body/eval_jaxpr/ppermute | solution.py:18
  453.5 39.5 %collective-permute-start = (bf16[512,2,128]{2,0,1:T(8,128)(2,1)}, bf16[512,2,128]{2,0,1:T(8,128)(2,1)}, u32[]{:S(2)}, u32[]{:S(2)}) collective-permute-start(bf16[512,2,128]{2,0,1:T(8,128)(2,1)} %copy.116), channel_id=1, source_target_pairs={{0,16},{16,32},{32,48},{48,64},{64,80},{80,96},{96,112},{112,128},... | collective-permute-start | bytes 786440 | tf_op jit(solution)/shard_map/while/body/eval_jaxpr/ppermute | solution.py:18
  477.6 15.9 %collective-permute-start.1 = (bf16[1,2,1601,128]{3,1,2,0:T(2,128)(2,1)}, bf16[1,2,1601,128]{3,1,2,0:T(2,128)(2,1)}, u32[]{:S(2)}, u32[]{:S(2)}) collective-permute-start(bf16[1,2,1601,128]{3,1,2,0:T(2,128)(2,1)} %copy.117), channel_id=1, source_target_pairs={{0,16},{16,32},{32,48},{48,64},{64,80},{80,96},{96,112},{112,128},... | collective-permute-start | bytes 2459144 | tf_op jit(solution)/shard_map/while/body/eval_jaxpr/ppermute | solution.py:18
  495.2 21.8 %collective-permute-start = (bf16[512,2,128]{2,0,1:T(8,128)(2,1)}, bf16[512,2,128]{2,0,1:T(8,128)(2,1)}, u32[]{:S(2)}, u32[]{:S(2)}) collective-permute-start(bf16[512,2,128]{2,0,1:T(8,128)(2,1)} %copy.116), channel_id=1, source_target_pairs={{0,16},{16,32},{32,48},{48,64},{64,80},{80,96},{96,112},{112,128},... | collective-permute-start | bytes 786440 | tf_op jit(solution)/shard_map/while/body/eval_jaxpr/ppermute | solution.py:18
  501.7 17.1 %collective-permute-start.1 = (bf16[1,2,1601,128]{3,1,2,0:T(2,128)(2,1)}, bf16[1,2,1601,128]{3,1,2,0:T(2,128)(2,1)}, u32[]{:S(2)}, u32[]{:S(2)}) collective-permute-start(bf16[1,2,1601,128]{3,1,2,0:T(2,128)(2,1)} %copy.117), channel_id=1, source_target_pairs={{0,16},{16,32},{32,48},{48,64},{64,80},{80,96},{96,112},{112,128},... | collective-permute-start | bytes 2459144 | tf_op jit(solution)/shard_map/while/body/eval_jaxpr/ppermute | solution.py:18
  520.5 26.6 %collective-permute-start = (bf16[512,2,128]{2,0,1:T(8,128)(2,1)}, bf16[512,2,128]{2,0,1:T(8,128)(2,1)}, u32[]{:S(2)}, u32[]{:S(2)}) collective-permute-start(bf16[512,2,128]{2,0,1:T(8,128)(2,1)} %copy.116), channel_id=1, source_target_pairs={{0,16},{16,32},{32,48},{48,64},{64,80},{80,96},{96,112},{112,128},... | collective-permute-start | bytes 786440 | tf_op jit(solution)/shard_map/while/body/eval_jaxpr/ppermute | solution.py:18
  525.0 34.0 %collective-permute-start.1 = (bf16[1,2,1601,128]{3,1,2,0:T(2,128)(2,1)}, bf16[1,2,1601,128]{3,1,2,0:T(2,128)(2,1)}, u32[]{:S(2)}, u32[]{:S(2)}) collective-permute-start(bf16[1,2,1601,128]{3,1,2,0:T(2,128)(2,1)} %copy.117), channel_id=1, source_target_pairs={{0,16},{16,32},{32,48},{48,64},{64,80},{80,96},{96,112},{112,128},... | collective-permute-start | bytes 2459144 | tf_op jit(solution)/shard_map/while/body/eval_jaxpr/ppermute | solution.py:18
  560.7 17.7 %collective-permute-start = (bf16[512,2,128]{2,0,1:T(8,128)(2,1)}, bf16[512,2,128]{2,0,1:T(8,128)(2,1)}, u32[]{:S(2)}, u32[]{:S(2)}) collective-permute-start(bf16[512,2,128]{2,0,1:T(8,128)(2,1)} %copy.116), channel_id=1, source_target_pairs={{0,16},{16,32},{32,48},{48,64},{64,80},{80,96},{96,112},{112,128},... | collective-permute-start | bytes 786440 | tf_op jit(solution)/shard_map/while/body/eval_jaxpr/ppermute | solution.py:18
  563.1 21.6 %collective-permute-start.1 = (bf16[1,2,1601,128]{3,1,2,0:T(2,128)(2,1)}, bf16[1,2,1601,128]{3,1,2,0:T(2,128)(2,1)}, u32[]{:S(2)}, u32[]{:S(2)}) collective-permute-start(bf16[1,2,1601,128]{3,1,2,0:T(2,128)(2,1)} %copy.117), channel_id=1, source_target_pairs={{0,16},{16,32},{32,48},{48,64},{64,80},{80,96},{96,112},{112,128},... | collective-permute-start | bytes 2459144 | tf_op jit(solution)/shard_map/while/body/eval_jaxpr/ppermute | solution.py:18
  585.9 1.6 copy-start.6
  604.7 1.0 copy-start.2
  604.7 1.1 copy-start.5
Sparse Core Ops, SparseCore 0:
  9.8 31.1 all-gather.2
  604.8 117.7 all-gather.4
where the time goes:
time: 754 us; the launch traced here: 745 us
  local copies, waits for them, and re-layouts  280 us (37%)
  waiting for transfers between devices  175 us (23%)
  starting transfers between devices  140 us (19%)
  loops' own time  45.8 us (6%)
  other arithmetic  33.7 us (4%)
  matrix products  31.7 us (4%)
  blocking collectives  24 us (3%)
  between operations  14.2 us (2%)
    ppermute x30, starting transfers between devices, shifted(): return lax.ppermute(value, axis, pairs)  140 us
    while x109, local copies, waits for them, and re-layouts  123 us
    all_gather x1, waiting for transfers between devices, joined(): everything = jax.tree.map(lambda part: lax.all_gather(part, axis), value)  91.3 us
    dynamic_slice x128, local copies, waits for them, and re-layouts, cross_update(): lax.scan(per_block, 0, (cross_queries, states[0], states[1], states[2], f...  76.9 us
    dynamic_update_slice x192, local copies, waits for them, and re-layouts, cross_update(): lax.scan(per_block, 0, (cross_queries, states[0], states[1], states[2], f...  58.6 us
    ppermute x30, waiting for transfers between devices, shifted(): return lax.ppermute(value, axis, pairs)  56.5 us
    another operation x16, loops' own time, cross_update(): lax.scan(per_block, 0, (cross_queries, states[0], states[1], states[2], f...  43.2 us
    all_gather x1, waiting for transfers between devices, per_device(): gathered = lax.all_gather(cross_query_columns, 'enc', axis=1, tiled=True)  27.4 us
  transfers between devices with their start and end apart: 32, of which 13 were waited for; matrix products, arithmetic and copies ran while one was open for 37% of the time, Pallas kernels for 0%

commit v1 on v0

v1 whole, which is shorter than its diff:
```python
import functools
import math

import jax
import jax.numpy as jnp
from jax import lax
from jax.experimental import pallas as pl
from jax.experimental.pallas import tpu as pltpu
from jax.sharding import PartitionSpec as P

MESH = pl.DeviceIdType.MESH
BF = jnp.bfloat16
F32 = jnp.float32
LAYERS = 8
ENC = 4
HEAD = 128
BLOCK = 128
ROWS = 512
TOKENS = 1601
HALF = 816
FIRST = 512
SECOND = 304
LAST_VALID = TOKENS - HALF - FIRST
NEG = -1e30
EXP_SCALE = math.log2(math.e) / math.sqrt(HEAD)
TILE = 512


def dot_t(a, b):
    return lax.dot_general(a, b, (((1,), (1,)), ((), ())), preferred_element_type=F32)


def weigh(p, v):
    ones = jnp.ones(v.shape, BF)
    return jnp.dot(p.astype(BF), jnp.concatenate([v, ones], axis=1), preferred_element_type=F32)


def kernel(
    sq_ref, text_ref, cq_ref, img_ref, seen_ref, owner_ref,
    self_out, cross_out,
    img_a, img_b, stage_a, stage_b, text, sq, cq, seen, seen_sm, pick, bias,
    acc, tot, top,
    s_part, s_lse, s_got, s_got_lse,
    c_part, c_lse, c_got, c_got_lse,
    za_s, za_r, zb_s, zb_r, tz_s, tz_r, ty_s, ty_r, y_s, y_r,
    sq_s, sq_r, cq_s, cq_r, so_s, so_r, sl_s, sl_r, co_s, co_r, cl_s, cl_r, local_sem,
):
    blk = lax.axis_index("blk")
    x = lax.axis_index("enc")
    z = blk // 2
    y = blk % 2
    partner = 2 * z + 1 - y

    def at(z_, y_, x_):
        return {"blk": 2 * z_ + y_, "enc": x_}

    def remote(src, dst, s, r, device):
        return pltpu.make_async_remote_copy(
            src_ref=src, dst_ref=dst, send_sem=s, recv_sem=r, device_id=device, device_id_type=MESH
        )

    sign = (1, -1)

    def layer(direction, distance):
        return (z - sign[direction] * distance + LAYERS) % LAYERS

    def onward(direction):
        return at((z + sign[direction] + LAYERS) % LAYERS, y, x)

    def unit(buf, s, r, direction, distance, order, sem):
        slot = 2 * layer(direction, distance) + (y + order) % 2
        return remote(
            buf.at[slot], buf.at[slot],
            s.at[direction, sem, order], r.at[direction, sem, order], onward(direction),
        )

    ring_a = (img_a, za_s, za_r)
    ring_b = (img_b, zb_s, zb_r)

    def send_own(ring, order):
        for direction in range(2):
            unit(*ring, direction, 0, order, 0).start()

    def ring_event(ring, distance, order):
        for direction in range(2):
            if distance == 4 and order != direction:
                continue
            unit(*ring, direction, distance, order, distance - 1).wait_recv()
            if distance < 3 or (distance == 3 and order == direction):
                unit(*ring, direction, distance, order, distance).start()

    def ring_last(ring):
        ring_event(ring, 4, 0)
        ring_event(ring, 4, 1)

    def ring_sent(ring):
        for direction in range(2):
            for distance in range(4):
                for order in range(2):
                    if distance < 3 or order == direction:
                        unit(*ring, direction, distance, order, distance).wait_send()

    def text_unit(direction, distance, sem):
        chunk = 2 * layer(direction, distance) + y
        return remote(
            text.at[chunk], text.at[chunk],
            tz_s.at[direction, sem], tz_r.at[direction, sem], onward(direction),
        )

    def text_across(chunk_layer, y_):
        chunk = 2 * chunk_layer + y_
        return remote(
            text.at[chunk], text.at[chunk], ty_s.at[chunk_layer], ty_r.at[chunk_layer],
            {"blk": partner},
        )

    def text_event(distance):
        for direction in range(2):
            if distance == 4 and direction == 1:
                continue
            text_unit(direction, distance, distance - 1).wait_recv()
            if distance < 3 or (distance == 3 and direction == 0):
                text_unit(direction, distance, distance).start()
            text_across(layer(direction, distance), y).start()

    def peer(step):
        return (x + step) % ENC

    def sq_copy(step):
        return remote(sq.at[x], sq.at[x], sq_s.at[step], sq_r.at[x], at(z, y, peer(step)))

    def cq_copy(flip, step):
        return remote(
            cq.at[x, y], cq.at[x, y], cq_s.at[flip, step], cq_r.at[x, y],
            at(z, (y + flip) % 2, peer(step)),
        )

    def half_copy(stage, buf, which):
        slot = 2 * z + y
        return remote(stage, buf.at[slot], y_s.at[which], y_r.at[which], {"blk": partner})

    def half_wait(stage, buf, which):
        slot = 2 * z + 1 - y
        remote(stage, buf.at[slot], y_s.at[which], y_r.at[which], {"blk": partner}).wait_recv()

    seen_copy = remote(seen.at[y], seen.at[y], y_s.at[2], y_r.at[2], {"blk": partner})

    def take_half(first, second, half):
        base = half * HALF
        for kv in range(2):
            first[kv] = img_ref[kv, base : base + FIRST, :]
            start = base + FIRST
            if half == 0:
                second[kv] = img_ref[kv, start : start + SECOND, :]
            else:
                whole = (LAST_VALID // 16) * 16
                second[kv, 0:whole, :] = img_ref[kv, start : start + whole, :]
                row = img_ref[kv, TOKENS - 1 : TOKENS, :].astype(F32)
                at_row = lax.broadcasted_iota(jnp.int32, (16, HEAD), 0)
                tail = jnp.where(at_row == 0, jnp.broadcast_to(row, (16, HEAD)), 0.0)
                second[kv, whole : whole + 16, :] = tail.astype(BF)
                second[kv, whole + 16 : SECOND, :] = jnp.zeros((SECOND - whole - 16, HEAD), BF)

    own = 2 * z + y
    for column in range(2):

        @pl.when(y == column)
        def _():
            take_half(img_a.at[own], img_b.at[own], column)
            take_half(stage_a, stage_b, 1 - column)

    text[own] = text_ref[...]
    sq[x] = sq_ref[...]
    cq[x, y] = cq_ref[...]
    seen[y] = jnp.zeros((8, 128), jnp.int32)
    seen[y, 0:4, 0:16] = seen_ref[...]

    barrier = pltpu.get_barrier_semaphore()
    for flip in range(2):
        for step in range(ENC):
            if flip or step:
                pl.semaphore_signal(
                    barrier, inc=1, device_id=at(z, (y + flip) % 2, peer(step)), device_id_type=MESH
                )
    for direction in range(2):
        pl.semaphore_signal(barrier, inc=1, device_id=onward(direction), device_id_type=MESH)
    pl.semaphore_wait(barrier, 9)

    for direction in range(2):
        text_unit(direction, 0, 0).start()
    half_copy(stage_a, img_a, 0).start()
    text_across(z, y).start()
    send_own(ring_a, 0)
    for step in (1, 3, 2):
        sq_copy(step).start()
    seen_copy.start()
    half_copy(stage_b, img_b, 1).start()
    for flip, step in ((0, 1), (0, 3), (1, 0), (0, 2), (1, 1), (1, 3), (1, 2)):
        cq_copy(flip, step).start()

    text_event(1)
    half_wait(stage_a, img_a, 0)
    send_own(ring_a, 1)
    text_event(2)
    ring_event(ring_a, 1, 0)
    text_event(3)
    text_event(4)
    ring_event(ring_a, 1, 1)
    ring_event(ring_a, 2, 0)
    for k in range(LAYERS):
        text_across(k, 1 - y).wait_recv()
    for step in (1, 2, 3):
        other = peer(step)
        remote(sq.at[other], sq.at[other], sq_s.at[step], sq_r.at[other], at(z, y, other)).wait_recv()

    diagonal = lax.broadcasted_iota(jnp.int32, (BLOCK, BLOCK), 0) == lax.broadcasted_iota(
        jnp.int32, (BLOCK, BLOCK), 1
    )

    def rows_of(ref, first_x, rows):
        return jnp.concatenate(
            [ref[first_x + k // 2, rows, (k % 2) * HEAD : (k % 2 + 1) * HEAD] for k in range(4)], axis=0
        )

    def put(part, lse, block, half, o, level):
        for k in range(4):
            t = 2 * half + k // 2
            lanes = slice((k % 2) * HEAD, (k % 2 + 1) * HEAD)
            part[block, t, :, lanes] = o[k * BLOCK : (k + 1) * BLOCK].astype(BF)
            square = jnp.where(diagonal, level[k * BLOCK : (k + 1) * BLOCK], 0.0)
            lse[block, t, k % 2 : k % 2 + 1, :] = jnp.sum(square, axis=0, keepdims=True)

    def s_copies(rb, step):
        t = peer(step)
        device = at(z, y, t)
        return (
            remote(s_part.at[rb, t], s_got.at[x, rb], so_s.at[rb, step], so_r.at[x, rb], device),
            remote(s_lse.at[rb, t], s_got_lse.at[x, rb], sl_s.at[rb, step], sl_r.at[x, rb], device),
        )

    def self_step(i):
        rb = i // 2
        half = i % 2
        rows = pl.ds(pl.multiple_of(rb * BLOCK, BLOCK), BLOCK)
        q = rows_of(sq, 2 * half, rows)
        keys = text[:, :, 0:HEAD].reshape(16 * BLOCK, HEAD)
        values = text[:, :, HEAD:].reshape(16 * BLOCK, HEAD)
        s = dot_t(q, keys)
        row = lax.broadcasted_iota(jnp.int32, (TILE, 1), 0) % BLOCK
        inside = jnp.where(x < rb, BLOCK, jnp.where(x == rb, row + 1, 0))
        limit = blk * BLOCK + inside
        index = lax.broadcasted_iota(jnp.int32, s.shape, 1)
        s = jnp.where(index < limit, s, NEG)
        m = jnp.max(s, axis=1, keepdims=True) * EXP_SCALE
        pv = weigh(jnp.exp2(s * EXP_SCALE - m), values)
        total = pv[:, HEAD:]
        put(s_part, s_lse, rb, half, pv[:, :HEAD] / total, m + jnp.log2(total))

        @pl.when(half == 1)
        def _():
            s_got[x, rb] = s_part[rb, x]
            s_got_lse[x, rb] = s_lse[rb, x]
            for step in (1, 3, 2):
                for copy in s_copies(rb, step):
                    copy.start()

    def self_loop(i, carry):
        @pl.when(i == 0)
        def _():
            ring_event(ring_a, 2, 1)

        @pl.when(i == 2)
        def _():
            ring_event(ring_a, 3, 0)
            send_own(ring_b, 0)

        @pl.when(i == 5)
        def _():
            ring_event(ring_a, 3, 1)
            half_wait(stage_b, img_b, 1)
            send_own(ring_b, 1)

        self_step(i)
        return carry

    lax.fori_loop(0, 8, self_loop, 0)
    ring_last(ring_a)

    remote(seen.at[1 - y], seen.at[1 - y], y_s.at[2], y_r.at[2], {"blk": partner}).wait_recv()
    to_scalar = pltpu.make_async_copy(seen, seen_sm, local_sem)
    to_scalar.start()
    to_scalar.wait()

    def choose(b, carry):
        latest = jnp.int32(0)
        earlier = jnp.int32(0)
        count = jnp.int32(0)
        for i in range(16):
            flag = seen_sm[b // 4, b % 4, i] > 0
            slot = owner_ref[i]
            earlier = jnp.where(jnp.logical_and(flag, count == 0), slot, earlier)
            latest = jnp.where(flag, slot, latest)
            count = count + jnp.where(flag, 1, 0)
        pick[b, 0] = latest
        pick[b, 1] = earlier
        bias[b] = jnp.where(count > 1, 0.0, NEG)
        return carry

    lax.fori_loop(0, 8, choose, 0)
    for flip in range(2):
        for step in range(ENC):
            if flip or step:
                ox, oy = peer(step), (y + flip) % 2
                remote(
                    cq.at[ox, oy], cq.at[ox, oy], cq_s.at[flip, step], cq_r.at[ox, oy], at(z, oy, ox)
                ).wait_recv()

    def cross_query(i):
        chunk = (i // 2) % 2
        rb = i // 4
        half = i % 2
        rows = pl.ds(pl.multiple_of(rb * BLOCK, BLOCK), BLOCK)
        q = jnp.concatenate(
            [
                cq[2 * half + k // 2, chunk, rows, (k % 2) * HEAD : (k % 2 + 1) * HEAD]
                for k in range(4)
            ],
            axis=0,
        )
        return chunk, rb, half, q

    def first_step(i):
        chunk, rb, half, q = cross_query(i)
        b = chunk * 4 + rb
        one, two, off = pick[b, 0], pick[b, 1], bias[b]
        s1 = dot_t(q, img_a[one, 0])
        s2 = dot_t(q, img_a[two, 0])
        m = jnp.maximum(
            jnp.max(s1, axis=1, keepdims=True) * EXP_SCALE,
            jnp.max(s2, axis=1, keepdims=True) * EXP_SCALE + off,
        )
        pv = weigh(jnp.exp2(s1 * EXP_SCALE - m), img_a[one, 1])
        pv = pv + weigh(jnp.exp2(s2 * EXP_SCALE - (m - off)), img_a[two, 1])
        acc[i] = pv[:, :HEAD]
        tot[i] = pv[:, HEAD:]
        top[i] = m

    def first_loop(i, carry):
        for k in range(5):

            @pl.when(i == 2 + 3 * k)
            def _():
                ring_event(ring_b, 1 + k // 2, k % 2)

        first_step(i)
        return carry

    lax.fori_loop(0, 16, first_loop, 0)

    def combine(got, got_lse, sources, block, out, rows):
        for hh in range(2):
            lanes = slice(hh * HEAD, (hh + 1) * HEAD)
            levels = []
            for k in range(sources):
                line = jnp.broadcast_to(got_lse[k, block, hh : hh + 1, :], (BLOCK, BLOCK))
                levels.append(jnp.sum(jnp.where(diagonal, line, 0.0), axis=1, keepdims=True))
            high = functools.reduce(jnp.maximum, levels)
            shares = [jnp.exp2(level - high) for level in levels]
            total = functools.reduce(jnp.add, shares)
            mixed = functools.reduce(
                jnp.add,
                [
                    got[k, block, :, lanes].astype(F32) * (share / total)
                    for k, share in enumerate(shares)
                ],
            )
            out[rows, lanes] = mixed.astype(BF)

    def self_combine(rb, carry):
        for step in (1, 2, 3):
            o = peer(step)
            device = at(z, y, o)
            remote(s_part.at[rb, o], s_got.at[o, rb], so_s.at[rb, step], so_r.at[o, rb], device).wait_recv()
            remote(s_lse.at[rb, o], s_got_lse.at[o, rb], sl_s.at[rb, step], sl_r.at[o, rb], device).wait_recv()
        combine(s_got, s_got_lse, 4, rb, self_out, pl.ds(pl.multiple_of(rb * BLOCK, BLOCK), BLOCK))
        return carry

    lax.fori_loop(0, 4, self_combine, 0)
    ring_event(ring_b, 3, 1)
    ring_last(ring_b)

    def c_copies(b, chunk, rb, step):
        t = peer(step)
        device = at(z, chunk, t)
        source = 2 * x + y
        return (
            remote(c_part.at[b, t], c_got.at[source, rb], co_s.at[b, step], co_r.at[source, rb], device),
            remote(c_lse.at[b, t], c_got_lse.at[source, rb], cl_s.at[b, step], cl_r.at[source, rb], device),
        )

    valid = jnp.where(y == 0, SECOND, LAST_VALID)

    def second_loop(i, carry):
        chunk, rb, half, q = cross_query(i)
        b = chunk * 4 + rb
        one, two, off = pick[b, 0], pick[b, 1], bias[b]
        keep = lax.broadcasted_iota(jnp.int32, (TILE, SECOND), 1) < valid
        s1 = jnp.where(keep, dot_t(q, img_b[one, 0]), NEG)
        s2 = jnp.where(keep, dot_t(q, img_b[two, 0]), NEG)
        before = top[i]
        m = jnp.maximum(
            jnp.max(s1, axis=1, keepdims=True) * EXP_SCALE,
            jnp.max(s2, axis=1, keepdims=True) * EXP_SCALE + off,
        )
        m = jnp.maximum(m, before)
        fade = jnp.exp2(before - m)
        pv = weigh(jnp.exp2(s1 * EXP_SCALE - m), img_b[one, 1])
        pv = pv + weigh(jnp.exp2(s2 * EXP_SCALE - (m - off)), img_b[two, 1])
        total = tot[i] * fade + pv[:, HEAD:]
        put(c_part, c_lse, b, half, (acc[i] * fade + pv[:, :HEAD]) / total, m + jnp.log2(total))

        @pl.when(half == 1)
        def _():
            for step in (2, 1, 3):
                for copy in c_copies(b, chunk, rb, step):
                    copy.start()

            @pl.when(chunk == y)
            def _():
                c_got[2 * x + y, rb] = c_part[b, x]
                c_got_lse[2 * x + y, rb] = c_lse[b, x]

            @pl.when(chunk != y)
            def _():
                for copy in c_copies(b, chunk, rb, 0):
                    copy.start()

        return carry

    lax.fori_loop(0, 16, second_loop, 0)

    def cross_combine(rb, carry):
        for flip in range(2):
            for step in range(ENC):
                if flip or step:
                    ox, oy = peer(step), (y + flip) % 2
                    o = 2 * ox + oy
                    device = at(z, oy, ox)
                    remote(
                        c_part.at[rb, ox], c_got.at[o, rb], co_s.at[rb, step], co_r.at[o, rb], device
                    ).wait_recv()
                    remote(
                        c_lse.at[rb, ox], c_got_lse.at[o, rb], cl_s.at[rb, step], cl_r.at[o, rb], device
                    ).wait_recv()
        combine(c_got, c_got_lse, 8, rb, cross_out, pl.ds(pl.multiple_of(rb * BLOCK, BLOCK), BLOCK))
        return carry

    lax.fori_loop(0, 4, cross_combine, 0)

    ring_sent(ring_a)
    ring_sent(ring_b)
    for direction in range(2):
        for distance in range(4):
            if distance < 3 or direction == 0:
                text_unit(direction, distance, distance).wait_send()
    for k in range(LAYERS):
        text_across(k, y).wait_send()
    half_copy(stage_a, img_a, 0).wait_send()
    half_copy(stage_b, img_b, 1).wait_send()
    seen_copy.wait_send()
    for step in (1, 2, 3):
        sq_copy(step).wait_send()
    for flip in range(2):
        for step in range(ENC):
            if flip or step:
                cq_copy(flip, step).wait_send()

    def results_sent(rb, carry):
        for step in (1, 2, 3):
            for copy in s_copies(rb, step):
                copy.wait_send()
            for chunk in range(2):
                for copy in c_copies(chunk * 4 + rb, chunk, rb, step):
                    copy.wait_send()
        for copy in c_copies((1 - y) * 4 + rb, 1 - y, rb, 0):
            copy.wait_send()
        return carry

    lax.fori_loop(0, 4, results_sent, 0)


def per_device(self_query, text_kv, cross_query, image_kv, block_images, image_owner):
    quarter = lax.dynamic_slice_in_dim(text_kv, lax.axis_index("enc") * BLOCK, BLOCK, 0)
    quarter = quarter.reshape(BLOCK, 2 * HEAD)
    vmem = pl.BlockSpec(memory_space=pltpu.VMEM)
    smem = pl.BlockSpec(memory_space=pltpu.SMEM)
    dma = pltpu.SemaphoreType.DMA
    out = jax.ShapeDtypeStruct((ROWS, 2 * HEAD), BF)
    return pl.pallas_call(
        kernel,
        out_shape=(out, out),
        in_specs=[vmem, vmem, vmem, vmem, vmem, smem],
        out_specs=(vmem, vmem),
        scratch_shapes=[
            pltpu.VMEM((16, 2, FIRST, HEAD), BF),
            pltpu.VMEM((16, 2, SECOND, HEAD), BF),
            pltpu.VMEM((2, FIRST, HEAD), BF),
            pltpu.VMEM((2, SECOND, HEAD), BF),
            pltpu.VMEM((16, BLOCK, 2 * HEAD), BF),
            pltpu.VMEM((ENC, ROWS, 2 * HEAD), BF),
            pltpu.VMEM((ENC, 2, ROWS, 2 * HEAD), BF),
            pltpu.VMEM((2, 8, 128), jnp.int32),
            pltpu.SMEM((2, 8, 128), jnp.int32),
            pltpu.SMEM((8, 2), jnp.int32),
            pltpu.SMEM((8,), F32),
            pltpu.VMEM((16, TILE, HEAD), F32),
            pltpu.VMEM((16, TILE, HEAD), F32),
            pltpu.VMEM((16, TILE, 1), F32),
            pltpu.VMEM((4, ENC, BLOCK, 2 * HEAD), BF),
            pltpu.VMEM((4, ENC, 8, HEAD), F32),
            pltpu.VMEM((ENC, 4, BLOCK, 2 * HEAD), BF),
            pltpu.VMEM((ENC, 4, 8, HEAD), F32),
            pltpu.VMEM((8, ENC, BLOCK, 2 * HEAD), BF),
            pltpu.VMEM((8, ENC, 8, HEAD), F32),
            pltpu.VMEM((8, 4, BLOCK, 2 * HEAD), BF),
            pltpu.VMEM((8, 4, 8, HEAD), F32),
            dma((2, 4, 2)), dma((2, 4, 2)), dma((2, 4, 2)), dma((2, 4, 2)),
            dma((2, 4)), dma((2, 4)), dma((LAYERS,)), dma((LAYERS,)),
            dma((3,)), dma((3,)),
            dma((ENC,)), dma((ENC,)), dma((2, ENC)), dma((ENC, 2)),
            dma((4, ENC)), dma((ENC, 4)), dma((4, ENC)), dma((ENC, 4)),
            dma((8, ENC)), dma((8, 4)), dma((8, ENC)), dma((8, 4)),
            dma,
        ],
        compiler_params=pltpu.CompilerParams(
            collective_id=0, has_side_effects=True, vmem_limit_bytes=60 * 2**20
        ),
        cost_estimate=pl.CostEstimate(
            flops=512 * 22_000_000, bytes_accessed=8_000_000, transcendentals=22_000_000
        ),
    )(self_query, quarter, cross_query, image_kv[0], block_images, image_owner)


def solution(mesh):
    spread = P("blk", ("tp", "enc"))
    return jax.shard_map(
        per_device,
        mesh=mesh,
        in_specs=(spread, P("blk", None, "tp"), spread, P("blk", None, "enc", "tp"), P("blk", None), P()),
        out_specs=(spread, spread),
        check_vma=False,
    )
```

time: 754 us -> 145 us (0.19)
  local copies, waits for them, and re-layouts: 280 us -> 6.2 us
  waiting for transfers between devices: 175 us -> 0 us
  starting transfers between devices: 140 us -> 0 us
  Pallas kernels: 0 us -> 136 us
  loops' own time: 45.8 us -> 0 us
  other arithmetic: 33.7 us -> 0 us
  matrix products: 31.7 us -> 0 us
  blocking collectives: 24 us -> 0 us
  between operations: 14.2 us -> 0.66 us
    ppermute x30 -> x0, starting transfers between devices: 140 us -> none  [shifted(): return lax.ppermute(value, axis, pairs)]
    pallas_call x0 -> x1, Pallas kernels: none -> 136 us  [per_device(): pl.pallas_call(kernel, out_shape=(out, out), in_specs=[vmem, vmem, vmem,...]
    while x110 -> x0, local copies, waits for them, and re-layouts: 124 us -> none
    all_gather x2 -> x0, waiting for transfers between devices: 119 us -> none  [the longest x1 91.3 us: joined(): everything = jax.tree.map(lambda part: lax.all_gather(part, axis), value)]
    dynamic_slice x131 -> x1, local copies, waits for them, and re-layouts: 77.7 us -> 0.05 us  [per_device(): lax.dynamic_slice_in_dim(text_kv, lax.axis_index('enc') * BLOCK, BLOCK, 0)]
    dynamic_update_slice x192 -> x0, local copies, waits for them, and re-layouts: 58.6 us -> none  [cross_update(): lax.scan(per_block, 0, (cross_queries, states[0], states[1], states[2], f...]
    ppermute x30 -> x0, waiting for transfers between devices: 56.5 us -> none  [shifted(): return lax.ppermute(value, axis, pairs)]
    another operation x98 -> x0, loops' own time: 45.8 us -> none  [the longest x16 43.2 us: cross_update(): lax.scan(per_block, 0, (cross_queries, states[0], states[1], states[2], f...]
  transfers between devices with their start and end apart: 32 -> 0, of which waited for: 13 -> 0; matrix products, arithmetic and copies ran while one was open for 37% -> 0% of each run, Pallas kernels for 0% -> 0%
where the time goes in v1:
time: 145 us; the launch traced here: 143 us
  Pallas kernels  136 us (94%)
  local copies, waits for them, and re-layouts  6.2 us (4%)
    pallas_call x1, Pallas kernels, per_device(): pl.pallas_call(kernel, out_shape=(out, out), in_specs=[vmem, vmem, vmem,...  136 us
    unnamed x8, local copies, waits for them, and re-layouts  6.15 us

profile of v1, /device:TPU:16, one launch (start us, length us, event | category | flops | bytes accessed | tf_op | source)
XLA Modules:
  0.0 143.1 jit_solution(2301895434000088031)
XLA Ops:
  0.6 0.0 copy-start
  0.6 0.9 copy-done
  1.6 0.6 copy.13
  2.3 2.1 %copy.12 = bf16[1,2,1601,128]{3,2,1,0:T(8,128)(2,1)} copy(bf16[1,2,1601,128]{3,1,2,0:T(2,128)(2,1)} %param.9) | data formatting | bytes 1639424 | tf_op args[3]
  4.4 136.2 %shard_map.77 = (bf16[512,256]{1,0:T(8,128)(2,1)}, bf16[512,256]{1,0:T(8,128)(2,1)}) custom-call(bf16[512,256]{1,0:T(8,128)(2,1)} %sq_ref.1, bf16[128,256]{1,0:T(8,128)(2,1)} %bitcast.9, bf16[512,256]{1,0:T(8,128)(2,1)} %cq_ref.1, bf16[2,1601,128]{2,1,0:T(8,128)(2,1)} %bitcast.7, s32[4,16]{1,0:T(4,128)} %seen_ref.1, s32[16]{0:T(128)} %owner_ref.1), custom_call_target="tpu_custom_call" | custom-call | flops 11264000000 | bytes 8000000 | tf_op jit(solution)/shard_map/pallas_call | solution.py:499
  140.7 0.0 copy-start.1
  140.7 1.7 %copy.16 = bf16[512,256]{1,0:T(8,128)(2,1)} copy(bf16[512,256]{1,0:T(8,128)(2,1)} %get-tuple-element.4) | data formatting | bytes 524288
  142.4 0.0 copy-done.1
  142.4 0.7 copy.17
  (1 shorter events, 0.0 us)
Async XLA Ops:
  0.6 1.0 copy-start
  140.7 1.7 %copy-start.1 = (bf16[512,256]{1,0:T(8,128)(2,1)S(1)}, bf16[512,256]{1,0:T(8,128)(2,1)}, u32[]{:S(2)}) copy-start(bf16[512,256]{1,0:T(8,128)(2,1)} %get-tuple-element.5) | copy-start | bytes 786436

commit v2 on v1

v2 whole, which is shorter than its diff:
```python
import functools
import math

import jax
import jax.numpy as jnp
from jax import lax
from jax.experimental import pallas as pl
from jax.experimental.pallas import tpu as pltpu
from jax.sharding import PartitionSpec as P

MESH = pl.DeviceIdType.MESH
BF = jnp.bfloat16
F32 = jnp.float32
LAYERS = 8
ENC = 4
HEAD = 128
BLOCK = 128
ROWS = 512
TOKENS = 1601
HALF = 816
FIRST = 512
SECOND = 304
WHOLE = 256
LAST_VALID = TOKENS - HALF - FIRST
NEG = -1e30
EXP_SCALE = math.log2(math.e) / math.sqrt(HEAD)
TILE = 256


def dot_t(a, b):
    return lax.dot_general(a, b, (((1,), (1,)), ((), ())), preferred_element_type=F32)


def weigh(p, v):
    ones = jnp.ones(v.shape, BF)
    return jnp.dot(p.astype(BF), jnp.concatenate([v, ones], axis=1), preferred_element_type=F32)


def kernel(
    sq_ref, text_ref, cq_ref, img_ref, seen_ref, owner_ref,
    self_out, cross_out,
    img_a, img_b, text, sq, cq, seen, seen_sm, pick, bias,
    acc, tot, top,
    s_part, s_lse, s_got, s_got_lse,
    c_part, c_lse, c_got, c_got_lse,
    za_s, za_r, zb_s, zb_r, tz_s, tz_r, ty_s, ty_r, y_s, y_r,
    sq_s, sq_r, cq_s, cq_r, so_s, so_r, sl_s, sl_r, co_s, co_r, cl_s, cl_r, local_sem, load_sem, store_sem, self_rows, cross_rows,
):
    blk = lax.axis_index("blk")
    x = lax.axis_index("enc")
    z = blk // 2
    y = blk % 2
    partner = 2 * z + 1 - y

    def at(z_, y_, x_):
        return {"blk": 2 * z_ + y_, "enc": x_}

    def remote(src, dst, s, r, device):
        return pltpu.make_async_remote_copy(
            src_ref=src, dst_ref=dst, send_sem=s, recv_sem=r, device_id=device, device_id_type=MESH
        )

    sign = (1, -1)

    def layer(direction, distance):
        return (z - sign[direction] * distance + LAYERS) % LAYERS

    def onward(direction):
        return at((z + sign[direction] + LAYERS) % LAYERS, y, x)

    def unit(buf, s, r, direction, distance, order, sem):
        slot = 2 * layer(direction, distance) + (y + order) % 2
        return remote(
            buf.at[slot], buf.at[slot],
            s.at[direction, sem, order], r.at[direction, sem, order], onward(direction),
        )

    ring_a = (img_a, za_s, za_r)
    ring_b = (img_b, zb_s, zb_r)

    def send_own(ring, order):
        for direction in range(2):
            unit(*ring, direction, 0, order, 0).start()

    def ring_event(ring, distance, order):
        for direction in range(2):
            if distance == 4 and order != direction:
                continue
            unit(*ring, direction, distance, order, distance - 1).wait_recv()
            if distance < 3 or (distance == 3 and order == direction):
                unit(*ring, direction, distance, order, distance).start()

    def ring_last(ring):
        ring_event(ring, 4, 0)
        ring_event(ring, 4, 1)

    def ring_sent(ring):
        for direction in range(2):
            for distance in range(4):
                for order in range(2):
                    if distance < 3 or order == direction:
                        unit(*ring, direction, distance, order, distance).wait_send()

    def text_unit(direction, distance, sem):
        chunk = 2 * layer(direction, distance) + y
        return remote(
            text.at[chunk], text.at[chunk],
            tz_s.at[direction, sem], tz_r.at[direction, sem], onward(direction),
        )

    def text_across(chunk_layer, y_):
        chunk = 2 * chunk_layer + y_
        return remote(
            text.at[chunk], text.at[chunk], ty_s.at[chunk_layer], ty_r.at[chunk_layer],
            {"blk": partner},
        )

    def text_event(distance):
        for direction in range(2):
            if distance == 4 and direction == 1:
                continue
            text_unit(direction, distance, distance - 1).wait_recv()
            if distance < 3 or (distance == 3 and direction == 0):
                text_unit(direction, distance, distance).start()
            text_across(layer(direction, distance), y).start()

    def peer(step):
        return (x + step) % ENC

    def sq_copy(step):
        return remote(sq_ref, sq.at[x], sq_s.at[step], sq_r.at[x], at(z, y, peer(step)))

    def cq_copy(flip, step):
        return remote(
            cq_ref, cq.at[x, y], cq_s.at[flip, step], cq_r.at[x, y],
            at(z, (y + flip) % 2, peer(step)),
        )

    def part(half, which):
        size = (FIRST, SECOND)[which]
        start = pl.multiple_of(half * HALF + which * FIRST, 16)
        return img_ref.at[:, pl.ds(start, size), :]

    def half_copy(buf, which):
        slot = 2 * z + y
        return remote(
            part(1 - y, which), buf.at[slot], y_s.at[which], y_r.at[which], {"blk": partner}
        )

    def half_wait(buf, which):
        slot = 2 * z + 1 - y
        remote(
            part(1 - y, which), buf.at[slot], y_s.at[which], y_r.at[which], {"blk": partner}
        ).wait_recv()

    seen_copy = remote(seen.at[y], seen.at[y], y_s.at[2], y_r.at[2], {"blk": partner})

    own = 2 * z + y
    loads = [
        pltpu.make_async_copy(src, dst, load_sem.at[k])
        for k, (src, dst) in enumerate(
            (
                (text_ref, text.at[own]),
                (part(y, 0), img_a.at[own]),
                (part(y, 1), img_b.at[own]),
                (sq_ref, sq.at[x]),
                (cq_ref, cq.at[x, y]),
            )
        )
    ]
    for load in loads:
        load.start()

    barrier = pltpu.get_barrier_semaphore()
    for flip in range(2):
        for step in range(ENC):
            if flip or step:
                pl.semaphore_signal(
                    barrier, inc=1, device_id=at(z, (y + flip) % 2, peer(step)), device_id_type=MESH
                )
    for direction in range(2):
        pl.semaphore_signal(barrier, inc=1, device_id=onward(direction), device_id_type=MESH)

    seen[y] = jnp.zeros((8, 128), jnp.int32)
    seen[y, 0:4, 0:16] = seen_ref[...]

    pl.semaphore_wait(barrier, 9)

    half_copy(img_a, 0).start()
    for load in loads:
        load.wait()
    for direction in range(2):
        text_unit(direction, 0, 0).start()
    send_own(ring_a, 0)
    for step in (1, 3, 2):
        sq_copy(step).start()
    text_event(1)
    half_wait(img_a, 0)
    send_own(ring_a, 1)
    text_across(z, y).start()
    seen_copy.start()
    half_copy(img_b, 1).start()
    text_event(2)
    ring_event(ring_a, 1, 0)
    cq_copy(1, 0).start()
    text_event(3)
    text_event(4)
    ring_event(ring_a, 1, 1)
    cq_copy(0, 1).start()
    cq_copy(0, 3).start()
    ring_event(ring_a, 2, 0)
    cq_copy(1, 1).start()
    for k in range(LAYERS):
        text_across(k, 1 - y).wait_recv()
    for step in (1, 2, 3):
        other = peer(step)
        remote(sq.at[other], sq.at[other], sq_s.at[step], sq_r.at[other], at(z, y, other)).wait_recv()

    diagonal = lax.broadcasted_iota(jnp.int32, (BLOCK, BLOCK), 0) == lax.broadcasted_iota(
        jnp.int32, (BLOCK, BLOCK), 1
    )

    def pair(ref, rows):
        return jnp.concatenate([ref[rows, 0:HEAD], ref[rows, HEAD : 2 * HEAD]], axis=0)

    def put(part, lse, block, t, weighted, total, level):
        for k in range(2):
            mine = slice(k * BLOCK, (k + 1) * BLOCK)
            part[block, t, :, k * HEAD : (k + 1) * HEAD] = weighted[mine].astype(BF)
            square = jnp.where(diagonal, level[mine], 0.0)
            lse[block, t, k : k + 1, :] = jnp.sum(square, axis=0, keepdims=True)
            square = jnp.where(diagonal, total[mine], 0.0)
            lse[block, t, 2 + k : 3 + k, :] = jnp.sum(square, axis=0, keepdims=True)

    def s_copies(rb, step):
        t = peer(step)
        device = at(z, y, t)
        return (
            remote(s_part.at[rb, t], s_got.at[x, rb], so_s.at[rb, step], so_r.at[x, rb], device),
            remote(s_lse.at[rb, t], s_got_lse.at[x, rb], sl_s.at[rb, step], sl_r.at[x, rb], device),
        )

    def self_step(rb):
        rows = pl.ds(pl.multiple_of(rb * BLOCK, BLOCK), BLOCK)
        keys = text[:, :, 0:HEAD].reshape(16 * BLOCK, HEAD)
        values = text[:, :, HEAD:].reshape(16 * BLOCK, HEAD)
        row = lax.broadcasted_iota(jnp.int32, (TILE, 1), 0) % BLOCK
        inside = jnp.where(x < rb, BLOCK, jnp.where(x == rb, row + 1, 0))
        limit = blk * BLOCK + inside
        for t in range(ENC):
            s = dot_t(pair(sq.at[t], rows), keys)
            index = lax.broadcasted_iota(jnp.int32, s.shape, 1)
            s = jnp.where(index < limit, s, NEG)
            m = jnp.max(s, axis=1, keepdims=True) * EXP_SCALE
            pv = weigh(jnp.exp2(s * EXP_SCALE - m), values)
            put(s_part, s_lse, rb, t, pv[:, :HEAD], pv[:, HEAD:], m)
        s_got[x, rb] = s_part[rb, x]
        s_got_lse[x, rb] = s_lse[rb, x]

    def self_loop(i, carry):
        @pl.when(i == 0)
        def _():
            ring_event(ring_a, 2, 1)
            cq_copy(1, 3).start()

        @pl.when(i == 2)
        def _():
            ring_event(ring_a, 3, 0)
            send_own(ring_b, 0)
            cq_copy(0, 2).start()

        @pl.when(i == 3)
        def _():
            ring_event(ring_a, 3, 1)
            half_wait(img_b, 1)
            send_own(ring_b, 1)
            cq_copy(1, 2).start()

        self_step(i)
        return carry

    lax.fori_loop(0, 4, self_loop, 0)
    ring_last(ring_a)

    remote(seen.at[1 - y], seen.at[1 - y], y_s.at[2], y_r.at[2], {"blk": partner}).wait_recv()
    to_scalar = pltpu.make_async_copy(seen, seen_sm, local_sem)
    to_scalar.start()
    to_scalar.wait()

    def choose(b, carry):
        latest = jnp.int32(0)
        earlier = jnp.int32(0)
        count = jnp.int32(0)
        for i in range(16):
            flag = seen_sm[b // 4, b % 4, i] > 0
            slot = owner_ref[i]
            earlier = jnp.where(jnp.logical_and(flag, count == 0), slot, earlier)
            latest = jnp.where(flag, slot, latest)
            count = count + jnp.where(flag, 1, 0)
        pick[b, 0] = latest
        pick[b, 1] = earlier
        bias[b] = jnp.where(count > 1, 0.0, NEG)
        return carry

    lax.fori_loop(0, 8, choose, 0)
    for flip in range(2):
        for step in range(ENC):
            if flip or step:
                ox, oy = peer(step), (y + flip) % 2
                remote(
                    cq.at[ox, oy], cq.at[ox, oy], cq_s.at[flip, step], cq_r.at[ox, oy], at(z, oy, ox)
                ).wait_recv()

    def first_step(i):
        chunk, rb = i % 2, i // 2
        b = chunk * 4 + rb
        rows = pl.ds(pl.multiple_of(rb * BLOCK, BLOCK), BLOCK)
        one, two, off = pick[b, 0], pick[b, 1], bias[b]
        for t in range(ENC):
            q = pair(cq.at[t, chunk], rows)
            s1 = dot_t(q, img_a[one, 0])
            s2 = dot_t(q, img_a[two, 0])
            m = jnp.maximum(
                jnp.max(s1, axis=1, keepdims=True) * EXP_SCALE,
                jnp.max(s2, axis=1, keepdims=True) * EXP_SCALE + off,
            )
            pv = weigh(jnp.exp2(s1 * EXP_SCALE - m), img_a[one, 1])
            pv = pv + weigh(jnp.exp2(s2 * EXP_SCALE - (m - off)), img_a[two, 1])
            acc[i, t] = pv[:, :HEAD]
            tot[i, t] = pv[:, HEAD:]
            top[i, t] = m

    def first_loop(i, carry):
        for k in range(5):

            @pl.when(i == 1 + k)
            def _():
                ring_event(ring_b, 1 + k // 2, k % 2)
                if k < 4:
                    for step in (1, 3, 2):
                        for copy in s_copies(k, step):
                            copy.start()

        first_step(i)
        return carry

    lax.fori_loop(0, 8, first_loop, 0)

    def store(rows, out, block, sem):
        place = pl.ds(pl.multiple_of(block * BLOCK, BLOCK), BLOCK)
        return pltpu.make_async_copy(rows.at[block], out.at[place, :], store_sem.at[sem])

    def combine(got, got_lse, sources, block, rows):
        stats = [got_lse[k, block] for k in range(sources)]
        levels = [stat[0:2] for stat in stats]
        high = functools.reduce(jnp.maximum, levels)
        shares = [jnp.exp2(level - high) for level in levels]
        total = functools.reduce(jnp.add, [s * stat[2:4] for s, stat in zip(shares, stats)])
        shares = [share / total for share in shares]
        for hh in range(2):
            lanes = slice(hh * HEAD, (hh + 1) * HEAD)
            mixed = jnp.zeros((BLOCK, HEAD), F32)
            for k in range(sources):
                line = jnp.broadcast_to(shares[k][hh : hh + 1], (BLOCK, BLOCK))
                share = jnp.sum(jnp.where(diagonal, line, 0.0), axis=1, keepdims=True)
                mixed = mixed + got[k, block, :, lanes].astype(F32) * share
            rows[block, :, lanes] = mixed.astype(BF)

    def self_combine(rb, carry):
        for step in (1, 2, 3):
            o = peer(step)
            device = at(z, y, o)
            remote(s_part.at[rb, o], s_got.at[o, rb], so_s.at[rb, step], so_r.at[o, rb], device).wait_recv()
            remote(s_lse.at[rb, o], s_got_lse.at[o, rb], sl_s.at[rb, step], sl_r.at[o, rb], device).wait_recv()
        combine(s_got, s_got_lse, 4, rb, self_rows)
        store(self_rows, self_out, rb, rb).start()
        return carry

    lax.fori_loop(0, 4, self_combine, 0)
    ring_event(ring_b, 3, 1)
    ring_last(ring_b)

    def c_copies(b, chunk, rb, step):
        t = peer(step)
        device = at(z, chunk, t)
        source = 2 * x + y
        return (
            remote(c_part.at[b, t], c_got.at[source, rb], co_s.at[b, step], co_r.at[source, rb], device),
            remote(c_lse.at[b, t], c_got_lse.at[source, rb], cl_s.at[b, step], cl_r.at[source, rb], device),
        )

    valid = jnp.where(y == 0, SECOND, LAST_VALID)

    def second_loop(i, carry):
        chunk, rb = i % 2, i // 2
        b = chunk * 4 + rb
        rows = pl.ds(pl.multiple_of(rb * BLOCK, BLOCK), BLOCK)
        one, two, off = pick[b, 0], pick[b, 1], bias[b]
        keep = lax.broadcasted_iota(jnp.int32, (TILE, SECOND - WHOLE), 1) < valid - WHOLE

        def scores(q, slot):
            s = dot_t(q, img_b[slot, 0])
            return jnp.concatenate([s[:, :WHOLE], jnp.where(keep, s[:, WHOLE:], NEG)], axis=1)

        for t in range(ENC):
            q = pair(cq.at[t, chunk], rows)
            s1 = scores(q, one)
            s2 = scores(q, two)
            before = top[i, t]
            m = jnp.maximum(
                jnp.max(s1, axis=1, keepdims=True) * EXP_SCALE,
                jnp.max(s2, axis=1, keepdims=True) * EXP_SCALE + off,
            )
            m = jnp.maximum(m, before)
            fade = jnp.exp2(before - m)
            pv = weigh(jnp.exp2(s1 * EXP_SCALE - m), img_b[one, 1])
            pv = pv + weigh(jnp.exp2(s2 * EXP_SCALE - (m - off)), img_b[two, 1])
            put(c_part, c_lse, b, t, acc[i, t] * fade + pv[:, :HEAD], tot[i, t] * fade + pv[:, HEAD:], m)

        for step in (2, 1, 3):
            for copy in c_copies(b, chunk, rb, step):
                copy.start()

        @pl.when(chunk == y)
        def _():
            c_got[2 * x + y, rb] = c_part[b, x]
            c_got_lse[2 * x + y, rb] = c_lse[b, x]

        @pl.when(chunk != y)
        def _():
            for copy in c_copies(b, chunk, rb, 0):
                copy.start()

        return carry

    lax.fori_loop(0, 8, second_loop, 0)

    def cross_combine(rb, carry):
        for flip in range(2):
            for step in range(ENC):
                if flip or step:
                    ox, oy = peer(step), (y + flip) % 2
                    o = 2 * ox + oy
                    device = at(z, oy, ox)
                    remote(
                        c_part.at[rb, ox], c_got.at[o, rb], co_s.at[rb, step], co_r.at[o, rb], device
                    ).wait_recv()
                    remote(
                        c_lse.at[rb, ox], c_got_lse.at[o, rb], cl_s.at[rb, step], cl_r.at[o, rb], device
                    ).wait_recv()
        combine(c_got, c_got_lse, 8, rb, cross_rows)
        store(cross_rows, cross_out, rb, 4 + rb).start()
        return carry

    lax.fori_loop(0, 4, cross_combine, 0)

    ring_sent(ring_a)
    ring_sent(ring_b)
    for direction in range(2):
        for distance in range(4):
            if distance < 3 or direction == 0:
                text_unit(direction, distance, distance).wait_send()
    for k in range(LAYERS):
        text_across(k, y).wait_send()
    half_copy(img_a, 0).wait_send()
    half_copy(img_b, 1).wait_send()
    seen_copy.wait_send()
    for step in (1, 2, 3):
        sq_copy(step).wait_send()
    for flip in range(2):
        for step in range(ENC):
            if flip or step:
                cq_copy(flip, step).wait_send()

    def results_sent(rb, carry):
        for step in (1, 2, 3):
            for copy in s_copies(rb, step):
                copy.wait_send()
            for chunk in range(2):
                for copy in c_copies(chunk * 4 + rb, chunk, rb, step):
                    copy.wait_send()
        for copy in c_copies((1 - y) * 4 + rb, 1 - y, rb, 0):
            copy.wait_send()
        return carry

    lax.fori_loop(0, 4, results_sent, 0)
    for rb in range(4):
        store(self_rows, self_out, rb, rb).wait()
        store(cross_rows, cross_out, rb, 4 + rb).wait()


def per_device(self_query, text_kv, cross_query, image_kv, block_images, image_owner):
    quarter = lax.dynamic_slice_in_dim(text_kv, lax.axis_index("enc") * BLOCK, BLOCK, 0)
    quarter = quarter.reshape(BLOCK, 2 * HEAD)
    image = jnp.pad(image_kv[0], ((0, 0), (0, 2 * HALF - TOKENS), (0, 0)))
    vmem = pl.BlockSpec(memory_space=pltpu.VMEM)
    hbm = pl.BlockSpec(memory_space=pl.ANY)
    smem = pl.BlockSpec(memory_space=pltpu.SMEM)
    dma = pltpu.SemaphoreType.DMA
    out = jax.ShapeDtypeStruct((ROWS, 2 * HEAD), BF)
    return pl.pallas_call(
        kernel,
        out_shape=(out, out),
        in_specs=[hbm, hbm, hbm, hbm, vmem, smem],
        out_specs=(hbm, hbm),
        scratch_shapes=[
            pltpu.VMEM((16, 2, FIRST, HEAD), BF),
            pltpu.VMEM((16, 2, SECOND, HEAD), BF),
            pltpu.VMEM((16, BLOCK, 2 * HEAD), BF),
            pltpu.VMEM((ENC, ROWS, 2 * HEAD), BF),
            pltpu.VMEM((ENC, 2, ROWS, 2 * HEAD), BF),
            pltpu.VMEM((2, 8, 128), jnp.int32),
            pltpu.SMEM((2, 8, 128), jnp.int32),
            pltpu.SMEM((8, 2), jnp.int32),
            pltpu.SMEM((8,), F32),
            pltpu.VMEM((8, ENC, TILE, HEAD), F32),
            pltpu.VMEM((8, ENC, TILE, HEAD), F32),
            pltpu.VMEM((8, ENC, TILE, 1), F32),
            pltpu.VMEM((4, ENC, BLOCK, 2 * HEAD), BF),
            pltpu.VMEM((4, ENC, 8, HEAD), F32),
            pltpu.VMEM((ENC, 4, BLOCK, 2 * HEAD), BF),
            pltpu.VMEM((ENC, 4, 8, HEAD), F32),
            pltpu.VMEM((8, ENC, BLOCK, 2 * HEAD), BF),
            pltpu.VMEM((8, ENC, 8, HEAD), F32),
            pltpu.VMEM((8, 4, BLOCK, 2 * HEAD), BF),
            pltpu.VMEM((8, 4, 8, HEAD), F32),
            dma((2, 4, 2)), dma((2, 4, 2)), dma((2, 4, 2)), dma((2, 4, 2)),
            dma((2, 4)), dma((2, 4)), dma((LAYERS,)), dma((LAYERS,)),
            dma((3,)), dma((3,)),
            dma((ENC,)), dma((ENC,)), dma((2, ENC)), dma((ENC, 2)),
            dma((4, ENC)), dma((ENC, 4)), dma((4, ENC)), dma((ENC, 4)),
            dma((8, ENC)), dma((8, 4)), dma((8, ENC)), dma((8, 4)),
            dma, dma((5,)), dma((8,)),
            pltpu.VMEM((4, BLOCK, 2 * HEAD), BF),
            pltpu.VMEM((4, BLOCK, 2 * HEAD), BF),
        ],
        compiler_params=pltpu.CompilerParams(
            collective_id=0, has_side_effects=True, vmem_limit_bytes=60 * 2**20
        ),
        cost_estimate=pl.CostEstimate(
            flops=512 * 22_000_000, bytes_accessed=8_000_000, transcendentals=22_000_000
        ),
    )(self_query, quarter, cross_query, image, block_images, image_owner)


def solution(mesh):
    spread = P("blk", ("tp", "enc"))
    return jax.shard_map(
        per_device,
        mesh=mesh,
        in_specs=(spread, P("blk", None, "tp"), spread, P("blk", None, "enc", "tp"), P("blk", None), P()),
        out_specs=(spread, spread),
        check_vma=False,
    )
```

time: 145 us -> 126 us (0.87); the launches traced: 143 us -> 126 us
  Pallas kernels: 136 us -> 119 us
    pallas_call x1, Pallas kernels: 136 us -> 119 us  [per_device(): pl.pallas_call(kernel, out_shape=(out, out), in_specs=[hbm, hbm, hbm, hbm...]
where the time goes in v2:
time: 126 us
  Pallas kernels  119 us (94%)
  local copies, waits for them, and re-layouts  6.27 us (5%)
    pallas_call x1, Pallas kernels, per_device(): pl.pallas_call(kernel, out_shape=(out, out), in_specs=[hbm, hbm, hbm, hbm...  119 us
    unnamed x8, local copies, waits for them, and re-layouts  5.25 us

profile of v2, /device:TPU:16, one launch (start us, length us, event | category | flops | bytes accessed | tf_op | source)
XLA Modules:
  0.0 126.1 jit_solution(2862399426576200011)
XLA Ops:
  0.6 0.0 copy-start
  0.6 0.9 copy-done
  1.6 0.6 copy.13
  2.3 1.3 copy.12
  3.5 1.0 pad.4.img_ref
  4.5 119.1 %shard_map.77 = (bf16[512,256]{1,0:T(8,128)(2,1)}, bf16[512,256]{1,0:T(8,128)(2,1)}) custom-call(bf16[512,256]{1,0:T(8,128)(2,1)} %sq_ref.1, bf16[128,256]{1,0:T(8,128)(2,1)} %bitcast.9, bf16[512,256]{1,0:T(8,128)(2,1)} %cq_ref.1, bf16[2,1632,128]{2,1,0:T(8,128)(2,1)} %pad.4.img_ref, s32[4,16]{1,0:T(4,128)} %seen_ref.1, s32[16]{0:T(128)} %owner_ref.1), custom_call_target="tpu_custom_call" | custom-call | flops 11264000000 | bytes 8000000 | tf_op jit(solution)/shard_map/pallas_call | solution.py:501
  123.7 0.0 copy-start.1
  123.7 1.7 %copy.16 = bf16[512,256]{1,0:T(8,128)(2,1)} copy(bf16[512,256]{1,0:T(8,128)(2,1)} %get-tuple-element.4) | data formatting | bytes 524288
  125.4 0.0 copy-done.1
  125.4 0.7 copy.17
  (1 shorter events, 0.0 us)
Async XLA Ops:
  0.6 1.0 copy-start
  123.7 1.7 %copy-start.1 = (bf16[512,256]{1,0:T(8,128)(2,1)S(1)}, bf16[512,256]{1,0:T(8,128)(2,1)}, u32[]{:S(2)}) copy-start(bf16[512,256]{1,0:T(8,128)(2,1)} %get-tuple-element.5) | copy-start | bytes 786436

commit v3 on v2

--- a/solution.py
+++ b/solution.py
@@ -18,10 +18,9 @@
 ROWS = 512
 TOKENS = 1601
 HALF = 816
-FIRST = 512
-SECOND = 304
-WHOLE = 256
-LAST_VALID = TOKENS - HALF - FIRST
+SIZES = (512, 304)
+STARTS = (0, 512)
+LAST_VALID = TOKENS - HALF - STARTS[1]
 NEG = -1e30
 EXP_SCALE = math.log2(math.e) / math.sqrt(HEAD)
 TILE = 256
@@ -38,8 +37,8 @@
 
 def kernel(
     sq_ref, text_ref, cq_ref, img_ref, seen_ref, owner_ref,
-    self_out, cross_out,
-    img_a, img_b, text, sq, cq, seen, seen_sm, pick, bias,
+    out_ref,
+    img_a, img_b, raw, raw_text, stage_a, stage_b, text, sq, cq, seen, seen_sm, pick, bias,
     acc, tot, top,
     s_part, s_lse, s_got, s_got_lse,
     c_part, c_lse, c_got, c_got_lse,
@@ -136,33 +135,28 @@
             at(z, (y + flip) % 2, peer(step)),
         )
 
-    def part(half, which):
-        size = (FIRST, SECOND)[which]
-        start = pl.multiple_of(half * HALF + which * FIRST, 16)
-        return img_ref.at[:, pl.ds(start, size), :]
-
-    def half_copy(buf, which):
-        slot = 2 * z + y
-        return remote(
-            part(1 - y, which), buf.at[slot], y_s.at[which], y_r.at[which], {"blk": partner}
-        )
-
-    def half_wait(buf, which):
-        slot = 2 * z + 1 - y
-        remote(
-            part(1 - y, which), buf.at[slot], y_s.at[which], y_r.at[which], {"blk": partner}
-        ).wait_recv()
+    stages = ((stage_a, img_a), (stage_b, img_b))
+
+    def half_copy(which, slot):
+        stage, buf = stages[which]
+        return remote(stage, buf.at[slot], y_s.at[which], y_r.at[which], {"blk": partner})
+
+    def half_send(which):
+        return half_copy(which, 2 * z + y)
+
+    def half_wait(which):
+        half_copy(which, 2 * z + 1 - y).wait_recv()
 
     seen_copy = remote(seen.at[y], seen.at[y], y_s.at[2], y_r.at[2], {"blk": partner})
 
     own = 2 * z + y
+    quarter = pl.ds(pl.multiple_of(x * BLOCK, BLOCK), BLOCK)
     loads = [
         pltpu.make_async_copy(src, dst, load_sem.at[k])
         for k, (src, dst) in enumerate(
             (
-                (text_ref, text.at[own]),
-                (part(y, 0), img_a.at[own]),
-                (part(y, 1), img_b.at[own]),
+                (img_ref, raw.at[pl.ds(0, TOKENS)]),
+                (text_ref.at[quarter], raw_text),
                 (sq_ref, sq.at[x]),
                 (cq_ref, cq.at[x, y]),
             )
@@ -170,6 +164,7 @@
     ]
     for load in loads:
         load.start()
+    raw[TOKENS:] = jnp.zeros((2 * HALF - TOKENS, 2, HEAD), BF)
 
     barrier = pltpu.get_barrier_semaphore()
     for flip in range(2):
@@ -181,25 +176,31 @@
     for direction in range(2):
         pl.semaphore_signal(barrier, inc=1, device_id=onward(direction), device_id_type=MESH)
 
+    for load in loads:
+        load.wait()
+    for kv in range(2):
+        text[own, :, kv * HEAD : (kv + 1) * HEAD] = raw_text[:, kv, :]
+        for which, (stage, buf) in enumerate(stages):
+            size = SIZES[which]
+            buf[own, kv] = raw[pl.ds(y * HALF + STARTS[which], size), kv, :]
+            stage[kv] = raw[pl.ds((1 - y) * HALF + STARTS[which], size), kv, :]
     seen[y] = jnp.zeros((8, 128), jnp.int32)
     seen[y, 0:4, 0:16] = seen_ref[...]
 
     pl.semaphore_wait(barrier, 9)
 
-    half_copy(img_a, 0).start()
-    for load in loads:
-        load.wait()
+    half_send(0).start()
     for direction in range(2):
         text_unit(direction, 0, 0).start()
     send_own(ring_a, 0)
     for step in (1, 3, 2):
         sq_copy(step).start()
     text_event(1)
-    half_wait(img_a, 0)
+    half_wait(0)
     send_own(ring_a, 1)
     text_across(z, y).start()
     seen_copy.start()
-    half_copy(img_b, 1).start()
+    half_send(1).start()
     text_event(2)
     ring_event(ring_a, 1, 0)
     cq_copy(1, 0).start()
@@ -247,13 +248,12 @@
         row = lax.broadcasted_iota(jnp.int32, (TILE, 1), 0) % BLOCK
         inside = jnp.where(x < rb, BLOCK, jnp.where(x == rb, row + 1, 0))
         limit = blk * BLOCK + inside
+        index = lax.broadcasted_iota(jnp.int32, (TILE, 16 * BLOCK), 1)
+        scores = [jnp.where(index < limit, dot_t(pair(sq.at[t], rows), keys), NEG) for t in range(ENC)]
+        tops = [jnp.max(s, axis=1, keepdims=True) * EXP_SCALE for s in scores]
+        mixed = [weigh(jnp.exp2(s * EXP_SCALE - m), values) for s, m in zip(scores, tops)]
         for t in range(ENC):
-            s = dot_t(pair(sq.at[t], rows), keys)
-            index = lax.broadcasted_iota(jnp.int32, s.shape, 1)
-            s = jnp.where(index < limit, s, NEG)
-            m = jnp.max(s, axis=1, keepdims=True) * EXP_SCALE
-            pv = weigh(jnp.exp2(s * EXP_SCALE - m), values)
-            put(s_part, s_lse, rb, t, pv[:, :HEAD], pv[:, HEAD:], m)
+            put(s_part, s_lse, rb, t, mixed[t][:, :HEAD], mixed[t][:, HEAD:], tops[t])
         s_got[x, rb] = s_part[rb, x]
         s_got_lse[x, rb] = s_lse[rb, x]
 
@@ -272,7 +272,7 @@
         @pl.when(i == 3)
         def _():
             ring_event(ring_a, 3, 1)
-            half_wait(img_b, 1)
+            half_wait(1)
             send_own(ring_b, 1)
             cq_copy(1, 2).start()
 
@@ -311,31 +311,48 @@
                     cq.at[ox, oy], cq.at[ox, oy], cq_s.at[flip, step], cq_r.at[ox, oy], at(z, oy, ox)
                 ).wait_recv()
 
-    def first_step(i):
+    def block_of(i):
         chunk, rb = i % 2, i // 2
         b = chunk * 4 + rb
         rows = pl.ds(pl.multiple_of(rb * BLOCK, BLOCK), BLOCK)
-        one, two, off = pick[b, 0], pick[b, 1], bias[b]
+        return chunk, rb, b, rows, pick[b, 0], pick[b, 1], bias[b]
+
+    def tops_of(scores):
+        return [
+            jnp.maximum(jnp.max(s1, axis=1, keepdims=True), jnp.max(s2, axis=1, keepdims=True))
+            for s1, s2 in scores
+        ]
+
+    def mix(scores, tops, v1, v2):
+        return [
+            weigh(jnp.exp2(s1 - m), v1) + weigh(jnp.exp2(s2 - m), v2)
+            for (s1, s2), m in zip(scores, tops)
+        ]
+
+    def first_step(i):
+        chunk, rb, b, rows, one, two, off = block_of(i)
+        k1, k2, v1, v2 = img_a[one, 0], img_a[two, 0], img_a[one, 1], img_a[two, 1]
+        queries = [pair(cq.at[t, chunk], rows) for t in range(ENC)]
+        scores = [(dot_t(q, k1) * EXP_SCALE, dot_t(q, k2) * EXP_SCALE + off) for q in queries]
+        tops = tops_of(scores)
+        mixed = mix(scores, tops, v1, v2)
         for t in range(ENC):
-            q = pair(cq.at[t, chunk], rows)
-            s1 = dot_t(q, img_a[one, 0])
-            s2 = dot_t(q, img_a[two, 0])
-            m = jnp.maximum(
-                jnp.max(s1, axis=1, keepdims=True) * EXP_SCALE,
-                jnp.max(s2, axis=1, keepdims=True) * EXP_SCALE + off,
-            )
-            pv = weigh(jnp.exp2(s1 * EXP_SCALE - m), img_a[one, 1])
-            pv = pv + weigh(jnp.exp2(s2 * EXP_SCALE - (m - off)), img_a[two, 1])
-            acc[i, t] = pv[:, :HEAD]
-            tot[i, t] = pv[:, HEAD:]
-            top[i, t] = m
+            acc[i, t] = mixed[t][:, :HEAD]
+            tot[i, t] = mixed[t][:, HEAD:]
+            top[i, t] = tops[t]
+
+    def pass_event(k):
+        if k < 6:
+            ring_event(ring_b, 1 + k // 2, k % 2)
+        else:
+            ring_last(ring_b)
 
     def first_loop(i, carry):
-        for k in range(5):
-
-            @pl.when(i == 1 + k)
+        for k in range(7):
+
+            @pl.when(i == k)
             def _():
-                ring_event(ring_b, 1 + k // 2, k % 2)
+                pass_event(k)
                 if k < 4:
                     for step in (1, 3, 2):
                         for copy in s_copies(k, step):
@@ -346,9 +363,9 @@
 
     lax.fori_loop(0, 8, first_loop, 0)
 
-    def store(rows, out, block, sem):
+    def store(rows, which, block, sem):
         place = pl.ds(pl.multiple_of(block * BLOCK, BLOCK), BLOCK)
-        return pltpu.make_async_copy(rows.at[block], out.at[place, :], store_sem.at[sem])
+        return pltpu.make_async_copy(rows.at[block], out_ref.at[which, place, :], store_sem.at[sem])
 
     def combine(got, got_lse, sources, block, rows):
         stats = [got_lse[k, block] for k in range(sources)]
@@ -373,12 +390,10 @@
             remote(s_part.at[rb, o], s_got.at[o, rb], so_s.at[rb, step], so_r.at[o, rb], device).wait_recv()
             remote(s_lse.at[rb, o], s_got_lse.at[o, rb], sl_s.at[rb, step], sl_r.at[o, rb], device).wait_recv()
         combine(s_got, s_got_lse, 4, rb, self_rows)
-        store(self_rows, self_out, rb, rb).start()
+        store(self_rows, 0, rb, rb).start()
         return carry
 
     lax.fori_loop(0, 4, self_combine, 0)
-    ring_event(ring_b, 3, 1)
-    ring_last(ring_b)
 
     def c_copies(b, chunk, rb, step):
         t = peer(step)
@@ -389,33 +404,25 @@
             remote(c_lse.at[b, t], c_got_lse.at[source, rb], cl_s.at[b, step], cl_r.at[source, rb], device),
         )
 
-    valid = jnp.where(y == 0, SECOND, LAST_VALID)
-
-    def second_loop(i, carry):
-        chunk, rb = i % 2, i // 2
-        b = chunk * 4 + rb
-        rows = pl.ds(pl.multiple_of(rb * BLOCK, BLOCK), BLOCK)
-        one, two, off = pick[b, 0], pick[b, 1], bias[b]
-        keep = lax.broadcasted_iota(jnp.int32, (TILE, SECOND - WHOLE), 1) < valid - WHOLE
-
-        def scores(q, slot):
-            s = dot_t(q, img_b[slot, 0])
-            return jnp.concatenate([s[:, :WHOLE], jnp.where(keep, s[:, WHOLE:], NEG)], axis=1)
-
+    valid = jnp.where(y == 0, SIZES[1], LAST_VALID)
+
+    def last_loop(i, carry):
+        chunk, rb, b, rows, one, two, off = block_of(i)
+        bias_one = jnp.where(lax.broadcasted_iota(jnp.int32, (1, SIZES[1]), 1) < valid, 0.0, NEG)
+        bias_two = bias_one + off
+        before = [top[i, t] for t in range(ENC)]
+        k1, k2, v1, v2 = img_b[one, 0], img_b[two, 0], img_b[one, 1], img_b[two, 1]
+        queries = [pair(cq.at[t, chunk], rows) for t in range(ENC)]
+        scores = [
+            (dot_t(q, k1) * EXP_SCALE + bias_one, dot_t(q, k2) * EXP_SCALE + bias_two) for q in queries
+        ]
+        tops = [jnp.maximum(m, old) for m, old in zip(tops_of(scores), before)]
+        mixed = mix(scores, tops, v1, v2)
+        fades = [jnp.exp2(old - m) for old, m in zip(before, tops)]
+        weighted = [acc[i, t] * fades[t] + mixed[t][:, :HEAD] for t in range(ENC)]
+        totals = [tot[i, t] * fades[t] + mixed[t][:, HEAD:] for t in range(ENC)]
         for t in range(ENC):
-            q = pair(cq.at[t, chunk], rows)
-            s1 = scores(q, one)
-            s2 = scores(q, two)
-            before = top[i, t]
-            m = jnp.maximum(
-                jnp.max(s1, axis=1, keepdims=True) * EXP_SCALE,
-                jnp.max(s2, axis=1, keepdims=True) * EXP_SCALE + off,
-            )
-            m = jnp.maximum(m, before)
-            fade = jnp.exp2(before - m)
-            pv = weigh(jnp.exp2(s1 * EXP_SCALE - m), img_b[one, 1])
-            pv = pv + weigh(jnp.exp2(s2 * EXP_SCALE - (m - off)), img_b[two, 1])
-            put(c_part, c_lse, b, t, acc[i, t] * fade + pv[:, :HEAD], tot[i, t] * fade + pv[:, HEAD:], m)
+            put(c_part, c_lse, b, t, weighted[t], totals[t], tops[t])
 
         for step in (2, 1, 3):
             for copy in c_copies(b, chunk, rb, step):
@@ -433,7 +440,7 @@
 
         return carry
 
-    lax.fori_loop(0, 8, second_loop, 0)
+    lax.fori_loop(0, 8, last_loop, 0)
 
     def cross_combine(rb, carry):
         for flip in range(2):
@@ -449,7 +456,7 @@
                         c_lse.at[rb, ox], c_got_lse.at[o, rb], cl_s.at[rb, step], cl_r.at[o, rb], device
                     ).wait_recv()
         combine(c_got, c_got_lse, 8, rb, cross_rows)
-        store(cross_rows, cross_out, rb, 4 + rb).start()
+        store(cross_rows, 1, rb, 4 + rb).start()
         return carry
 
     lax.fori_loop(0, 4, cross_combine, 0)
@@ -462,8 +469,8 @@
                 text_unit(direction, distance, distance).wait_send()
     for k in range(LAYERS):
         text_across(k, y).wait_send()
-    half_copy(img_a, 0).wait_send()
-    half_copy(img_b, 1).wait_send()
+    for which in range(2):
+        half_send(which).wait_send()
     seen_copy.wait_send()
     for step in (1, 2, 3):
         sq_copy(step).wait_send()
@@ -485,27 +492,26 @@
 
     lax.fori_loop(0, 4, results_sent, 0)
     for rb in range(4):
-        store(self_rows, self_out, rb, rb).wait()
-        store(cross_rows, cross_out, rb, 4 + rb).wait()
+        store(self_rows, 0, rb, rb).wait()
+        store(cross_rows, 1, rb, 4 + rb).wait()
 
 
 def per_device(self_query, text_kv, cross_query, image_kv, block_images, image_owner):
-    quarter = lax.dynamic_slice_in_dim(text_kv, lax.axis_index("enc") * BLOCK, BLOCK, 0)
-    quarter = quarter.reshape(BLOCK, 2 * HEAD)
-    image = jnp.pad(image_kv[0], ((0, 0), (0, 2 * HALF - TOKENS), (0, 0)))
+    image = jnp.swapaxes(image_kv[0], 0, 1)
     vmem = pl.BlockSpec(memory_space=pltpu.VMEM)
     hbm = pl.BlockSpec(memory_space=pl.ANY)
     smem = pl.BlockSpec(memory_space=pltpu.SMEM)
     dma = pltpu.SemaphoreType.DMA
-    out = jax.ShapeDtypeStruct((ROWS, 2 * HEAD), BF)
-    return pl.pallas_call(
+    both = pl.pallas_call(
         kernel,
-        out_shape=(out, out),
+        out_shape=jax.ShapeDtypeStruct((2, ROWS, 2 * HEAD), BF),
         in_specs=[hbm, hbm, hbm, hbm, vmem, smem],
-        out_specs=(hbm, hbm),
+        out_specs=hbm,
         scratch_shapes=[
-            pltpu.VMEM((16, 2, FIRST, HEAD), BF),
-            pltpu.VMEM((16, 2, SECOND, HEAD), BF),
+            *(pltpu.VMEM((16, 2, size, HEAD), BF) for size in SIZES),
+            pltpu.VMEM((2 * HALF, 2, HEAD), BF),
+            pltpu.VMEM((BLOCK, 2, HEAD), BF),
+            *(pltpu.VMEM((2, size, HEAD), BF) for size in SIZES),
             pltpu.VMEM((16, BLOCK, 2 * HEAD), BF),
             pltpu.VMEM((ENC, ROWS, 2 * HEAD), BF),
             pltpu.VMEM((ENC, 2, ROWS, 2 * HEAD), BF),
@@ -530,7 +536,7 @@
             dma((ENC,)), dma((ENC,)), dma((2, ENC)), dma((ENC, 2)),
             dma((4, ENC)), dma((ENC, 4)), dma((4, ENC)), dma((ENC, 4)),
             dma((8, ENC)), dma((8, 4)), dma((8, ENC)), dma((8, 4)),
-            dma, dma((5,)), dma((8,)),
+            dma, dma((4,)), dma((8,)),
             pltpu.VMEM((4, BLOCK, 2 * HEAD), BF),
             pltpu.VMEM((4, BLOCK, 2 * HEAD), BF),
         ],
@@ -540,7 +546,8 @@
         cost_estimate=pl.CostEstimate(
             flops=512 * 22_000_000, bytes_accessed=8_000_000, transcendentals=22_000_000
         ),
-    )(self_query, quarter, cross_query, image, block_images, image_owner)
+    )(self_query, text_kv, cross_query, image, block_images, image_owner)
+    return both[0], both[1]
 
 
 def solution(mesh):

time: 126 us -> 120 us (0.952)
  local copies, waits for them, and re-layouts: 6.27 us -> 1.85 us
  Pallas kernels: 119 us -> 117 us
    unnamed x8 -> x0, local copies, waits for them, and re-layouts: 5.25 us -> none
    pallas_call x1, Pallas kernels: 119 us -> 117 us  [per_device(): pl.pallas_call(kernel, out_shape=jax.ShapeDtypeStruct((2, ROWS, 2 * HEAD)...]
    squeeze x0 -> x1, local copies, waits for them, and re-layouts: none -> 1.85 us  [per_device(): return (both[0], both[1])]
where the time goes in v3:
time: 120 us; the launch traced here: 119 us
  Pallas kernels  117 us (98%)
  local copies, waits for them, and re-layouts  1.85 us (2%)
    pallas_call x1, Pallas kernels, per_device(): pl.pallas_call(kernel, out_shape=jax.ShapeDtypeStruct((2, ROWS, 2 * HEAD)...  117 us

profile of v3, /device:TPU:16, one launch (start us, length us, event | category | flops | bytes accessed | tf_op | source)
XLA Modules:
  0.0 119.0 jit_solution(12693258315810393483)
XLA Ops:
  0.6 116.6 %shard_map.77 = bf16[2,512,256]{2,1,0:T(8,128)(2,1)} custom-call(bf16[512,256]{1,0:T(8,128)(2,1)} %sq_ref.1, bf16[512,2,128]{2,1,0:T(2,128)(2,1)} %text_ref.1, bf16[512,256]{1,0:T(8,128)(2,1)} %cq_ref.1, bf16[1601,2,128]{2,1,0:T(2,128)(2,1)} %bitcast.7, s32[4,16]{1,0:T(4,128)} %seen_ref.1, s32[16]{0:T(128)} %owner_ref.1), custom_call_target="tpu_custom_call" | custom-call | flops 11264000000 | bytes 8000000 | tf_op jit(solution)/shard_map/pallas_call | solution.py:505
  117.2 1.9 %slice_bitcast_fusion = (bf16[512,256]{1,0:T(8,128)(2,1)}, bf16[512,256]{1,0:T(8,128)(2,1)}) fusion(bf16[2,512,256]{2,1,0:T(8,128)(2,1)} %shard_map.77), kind=kLoop, calls=%fused_computation | loop fusion | bytes 1048576 | tf_op jit(solution)/shard_map/squeeze | solution.py:550

commit v4 on v3

--- a/solution.py
+++ b/solution.py
@@ -42,8 +42,10 @@
     acc, tot, top,
     s_part, s_lse, s_got, s_got_lse,
     c_part, c_lse, c_got, c_got_lse,
+    over, over_lse, side, side_lse, joint, joint_lse,
     za_s, za_r, zb_s, zb_r, tz_s, tz_r, ty_s, ty_r, y_s, y_r,
-    sq_s, sq_r, cq_s, cq_r, so_s, so_r, sl_s, sl_r, co_s, co_r, cl_s, cl_r, local_sem, load_sem, store_sem, self_rows, cross_rows,
+    sq_s, sq_r, cq_s, cq_r, so_s, so_r, sl_s, sl_r, co_s, co_r, cl_s, cl_r,
+    oo_s, oo_r, ol_s, ol_r, do_s, do_r, dl_s, dl_r, jo_s, jo_r, jl_s, jl_r, local_sem, load_sem, store_sem, self_rows, cross_rows,
 ):
     blk = lax.axis_index("blk")
     x = lax.axis_index("enc")
@@ -350,7 +352,7 @@
     def first_loop(i, carry):
         for k in range(7):
 
-            @pl.when(i == k)
+            @pl.when(i == k + 1)
             def _():
                 pass_event(k)
                 if k < 4:
@@ -367,21 +369,33 @@
         place = pl.ds(pl.multiple_of(block * BLOCK, BLOCK), BLOCK)
         return pltpu.make_async_copy(rows.at[block], out_ref.at[which, place, :], store_sem.at[sem])
 
-    def combine(got, got_lse, sources, block, rows):
-        stats = [got_lse[k, block] for k in range(sources)]
+    def blend(parts, stats, out, stat_out):
+        stats = [stat[...] for stat in stats]
         levels = [stat[0:2] for stat in stats]
         high = functools.reduce(jnp.maximum, levels)
         shares = [jnp.exp2(level - high) for level in levels]
         total = functools.reduce(jnp.add, [s * stat[2:4] for s, stat in zip(shares, stats)])
-        shares = [share / total for share in shares]
+        if stat_out is None:
+            shares = [share / total for share in shares]
+        else:
+            stat_out[0:2, :] = high
+            stat_out[2:4, :] = total
         for hh in range(2):
             lanes = slice(hh * HEAD, (hh + 1) * HEAD)
             mixed = jnp.zeros((BLOCK, HEAD), F32)
-            for k in range(sources):
-                line = jnp.broadcast_to(shares[k][hh : hh + 1], (BLOCK, BLOCK))
-                share = jnp.sum(jnp.where(diagonal, line, 0.0), axis=1, keepdims=True)
-                mixed = mixed + got[k, block, :, lanes].astype(F32) * share
-            rows[block, :, lanes] = mixed.astype(BF)
+            for part, share in zip(parts, shares):
+                line = jnp.broadcast_to(share[hh : hh + 1], (BLOCK, BLOCK))
+                column = jnp.sum(jnp.where(diagonal, line, 0.0), axis=1, keepdims=True)
+                mixed = mixed + part[:, lanes].astype(F32) * column
+            out[:, lanes] = mixed.astype(BF)
+
+    def combine(got, got_lse, sources, block, rows):
+        blend(
+            [got.at[k, block] for k in range(sources)],
+            [got_lse.at[k, block] for k in range(sources)],
+            rows.at[block],
+            None,
+        )
 
     def self_combine(rb, carry):
         for step in (1, 2, 3):
@@ -395,19 +409,87 @@
 
     lax.fori_loop(0, 4, self_combine, 0)
 
-    def c_copies(b, chunk, rb, step):
-        t = peer(step)
-        device = at(z, chunk, t)
-        source = 2 * x + y
-        return (
-            remote(c_part.at[b, t], c_got.at[source, rb], co_s.at[b, step], co_r.at[source, rb], device),
-            remote(c_lse.at[b, t], c_got_lse.at[source, rb], cl_s.at[b, step], cl_r.at[source, rb], device),
-        )
+    def pairs(src, src_lse, dst, dst_lse, so, ro, sl, rl, device):
+        return (remote(src, dst, so, ro, device), remote(src_lse, dst_lse, sl, rl, device))
+
+    def own_copies(rb, step, source):
+        t, b = peer(step), 4 * y + rb
+        return pairs(
+            c_part.at[b, t], c_lse.at[b, t], c_got.at[source, rb], c_got_lse.at[source, rb],
+            co_s.at[rb, step], co_r.at[source, rb], cl_s.at[rb, step], cl_r.at[source, rb], at(z, y, t),
+        )
+
+    def side_copies(rb, step, source):
+        t, b = peer(step), 4 * (1 - y) + rb
+        return pairs(
+            c_part.at[b, t], c_lse.at[b, t], side.at[source, rb], side_lse.at[source, rb],
+            do_s.at[rb, step], do_r.at[source, rb], dl_s.at[rb, step], dl_r.at[source, rb], at(z, y, t),
+        )
+
+    def over_copies(rb):
+        b, k = 4 * (1 - y) + rb, rb - 2
+        return pairs(
+            c_part.at[b], c_lse.at[b], over.at[k], over_lse.at[k],
+            oo_s.at[k], oo_r.at[k], ol_s.at[k], ol_r.at[k], {"blk": partner},
+        )
+
+    def joint_copies(rb):
+        return pairs(
+            joint.at[rb], joint_lse.at[rb], c_got.at[ENC, rb], c_got_lse.at[ENC, rb],
+            jo_s.at[rb], jo_r.at[rb], jl_s.at[rb], jl_r.at[rb], {"blk": partner},
+        )
+
+    def start_own(rb):
+        b = 4 * y + rb
+        for step in (2, 1, 3):
+            for copy in own_copies(rb, step, x):
+                copy.start()
+        c_got[x, rb] = c_part[b, x]
+        c_got_lse[x, rb] = c_lse[b, x]
+
+    def start_side(rb):
+        for step in (2, 1, 3):
+            for copy in side_copies(rb, step, x):
+                copy.start()
+        b = 4 * (1 - y) + rb
+        side[x, rb] = c_part[b, x]
+        side_lse[x, rb] = c_lse[b, x]
+
+    def start_joint(rb):
+        for step in (1, 2, 3):
+            for copy in side_copies(rb, step, peer(step)):
+                copy.wait_recv()
+        blend(
+            [side.at[k, rb] for k in range(ENC)],
+            [side_lse.at[k, rb] for k in range(ENC)],
+            joint.at[rb],
+            joint_lse.at[rb],
+        )
+        for copy in joint_copies(rb):
+            copy.start()
+
+    def add_over(rb):
+        b, k = 4 * y + rb, rb - 2
+        for copy in over_copies(rb):
+            copy.wait_recv()
+        for t in range(ENC):
+            blend(
+                [c_part.at[b, t], over.at[k, t]],
+                [c_lse.at[b, t], over_lse.at[k, t]],
+                c_part.at[b, t],
+                c_lse.at[b, t],
+            )
 
     valid = jnp.where(y == 0, SIZES[1], LAST_VALID)
 
-    def last_loop(i, carry):
-        chunk, rb, b, rows, one, two, off = block_of(i)
+    def last_loop(j, carry):
+        mine = j // 4
+        rb = (1 - mine) * (j // 2 + 2 * (j % 2)) + mine * (j % 4)
+        chunk = (1 - mine) * (1 - y) + mine * y
+        i = 2 * rb + chunk
+        b = 4 * chunk + rb
+        rows = pl.ds(pl.multiple_of(rb * BLOCK, BLOCK), BLOCK)
+        one, two, off = pick[b, 0], pick[b, 1], bias[b]
         bias_one = jnp.where(lax.broadcasted_iota(jnp.int32, (1, SIZES[1]), 1) < valid, 0.0, NEG)
         bias_two = bias_one + off
         before = [top[i, t] for t in range(ENC)]
@@ -424,42 +506,54 @@
         for t in range(ENC):
             put(c_part, c_lse, b, t, weighted[t], totals[t], tops[t])
 
-        for step in (2, 1, 3):
-            for copy in c_copies(b, chunk, rb, step):
-                copy.start()
-
-        @pl.when(chunk == y)
+        for k in (0, 2):
+
+            @pl.when(j == k)
+            def _():
+                start_side(k // 2)
+
+        for k in (1, 3):
+
+            @pl.when(j == k)
+            def _():
+                for copy in over_copies(2 + k // 2):
+                    copy.start()
+
+        for k in (4, 5):
+
+            @pl.when(j == k)
+            def _():
+                start_own(k - 4)
+
+        for k in (3, 5):
+
+            @pl.when(j == k)
+            def _():
+                start_joint(k // 2 - 1)
+
+        @pl.when(j >= 6)
         def _():
-            c_got[2 * x + y, rb] = c_part[b, x]
-            c_got_lse[2 * x + y, rb] = c_lse[b, x]
-
-        @pl.when(chunk != y)
-        def _():
-            for copy in c_copies(b, chunk, rb, 0):
-                copy.start()
+            add_over(j - 4)
+            start_own(j - 4)
 
         return carry
 
     lax.fori_loop(0, 8, last_loop, 0)
 
-    def cross_combine(rb, carry):
-        for flip in range(2):
-            for step in range(ENC):
-                if flip or step:
-                    ox, oy = peer(step), (y + flip) % 2
-                    o = 2 * ox + oy
-                    device = at(z, oy, ox)
-                    remote(
-                        c_part.at[rb, ox], c_got.at[o, rb], co_s.at[rb, step], co_r.at[o, rb], device
-                    ).wait_recv()
-                    remote(
-                        c_lse.at[rb, ox], c_got_lse.at[o, rb], cl_s.at[rb, step], cl_r.at[o, rb], device
-                    ).wait_recv()
-        combine(c_got, c_got_lse, 8, rb, cross_rows)
+    def cross_combine(rb, sources):
+        for step in (1, 2, 3):
+            for copy in own_copies(rb, step, peer(step)):
+                copy.wait_recv()
+        if sources > ENC:
+            for copy in joint_copies(rb):
+                copy.wait_recv()
+        combine(c_got, c_got_lse, sources, rb, cross_rows)
         store(cross_rows, 1, rb, 4 + rb).start()
-        return carry
-
-    lax.fori_loop(0, 4, cross_combine, 0)
+
+    for rb in (0, 1):
+        cross_combine(rb, ENC + 1)
+    for rb in (2, 3):
+        cross_combine(rb, ENC)
 
     ring_sent(ring_a)
     ring_sent(ring_b)
@@ -479,18 +573,17 @@
             if flip or step:
                 cq_copy(flip, step).wait_send()
 
-    def results_sent(rb, carry):
+    for rb in range(4):
         for step in (1, 2, 3):
             for copy in s_copies(rb, step):
                 copy.wait_send()
-            for chunk in range(2):
-                for copy in c_copies(chunk * 4 + rb, chunk, rb, step):
+            for copy in own_copies(rb, step, x):
+                copy.wait_send()
+            if rb < 2:
+                for copy in side_copies(rb, step, x):
                     copy.wait_send()
-        for copy in c_copies((1 - y) * 4 + rb, 1 - y, rb, 0):
+        for copy in joint_copies(rb) if rb < 2 else over_copies(rb):
             copy.wait_send()
-        return carry
-
-    lax.fori_loop(0, 4, results_sent, 0)
     for rb in range(4):
         store(self_rows, 0, rb, rb).wait()
         store(cross_rows, 1, rb, 4 + rb).wait()
@@ -528,14 +621,23 @@
             pltpu.VMEM((ENC, 4, 8, HEAD), F32),
             pltpu.VMEM((8, ENC, BLOCK, 2 * HEAD), BF),
             pltpu.VMEM((8, ENC, 8, HEAD), F32),
-            pltpu.VMEM((8, 4, BLOCK, 2 * HEAD), BF),
-            pltpu.VMEM((8, 4, 8, HEAD), F32),
+            pltpu.VMEM((ENC + 1, 4, BLOCK, 2 * HEAD), BF),
+            pltpu.VMEM((ENC + 1, 4, 8, HEAD), F32),
+            pltpu.VMEM((2, ENC, BLOCK, 2 * HEAD), BF),
+            pltpu.VMEM((2, ENC, 8, HEAD), F32),
+            pltpu.VMEM((ENC, 2, BLOCK, 2 * HEAD), BF),
+            pltpu.VMEM((ENC, 2, 8, HEAD), F32),
+            pltpu.VMEM((2, BLOCK, 2 * HEAD), BF),
+            pltpu.VMEM((2, 8, HEAD), F32),
             dma((2, 4, 2)), dma((2, 4, 2)), dma((2, 4, 2)), dma((2, 4, 2)),
             dma((2, 4)), dma((2, 4)), dma((LAYERS,)), dma((LAYERS,)),
             dma((3,)), dma((3,)),
             dma((ENC,)), dma((ENC,)), dma((2, ENC)), dma((ENC, 2)),
             dma((4, ENC)), dma((ENC, 4)), dma((4, ENC)), dma((ENC, 4)),
-            dma((8, ENC)), dma((8, 4)), dma((8, ENC)), dma((8, 4)),
+            dma((4, ENC)), dma((ENC, 4)), dma((4, ENC)), dma((ENC, 4)),
+            dma((2,)), dma((2,)), dma((2,)), dma((2,)),
+            dma((2, ENC)), dma((ENC, 2)), dma((2, ENC)), dma((ENC, 2)),
+            dma((2,)), dma((2,)), dma((2,)), dma((2,)),
             dma, dma((4,)), dma((8,)),
             pltpu.VMEM((4, BLOCK, 2 * HEAD), BF),
             pltpu.VMEM((4, BLOCK, 2 * HEAD), BF),

time: 120 us -> 114 us (0.950)
  Pallas kernels: 117 us -> 111 us
    pallas_call x1, Pallas kernels: 117 us -> 111 us  [per_device(): pl.pallas_call(kernel, out_shape=jax.ShapeDtypeStruct((2, ROWS, 2 * HEAD)...]
where the time goes in v4:
time: 114 us; the launch traced here: 113 us
  Pallas kernels  111 us (97%)
  local copies, waits for them, and re-layouts  1.85 us (2%)
    pallas_call x1, Pallas kernels, per_device(): pl.pallas_call(kernel, out_shape=jax.ShapeDtypeStruct((2, ROWS, 2 * HEAD)...  111 us

profile of v4, /device:TPU:16, one launch (start us, length us, event | category | flops | bytes accessed | tf_op | source)
XLA Modules:
  0.0 113.2 jit_solution(5122356262134889567)
XLA Ops:
  0.6 110.7 %shard_map.77 = bf16[2,512,256]{2,1,0:T(8,128)(2,1)} custom-call(bf16[512,256]{1,0:T(8,128)(2,1)} %sq_ref.1, bf16[512,2,128]{2,1,0:T(2,128)(2,1)} %text_ref.1, bf16[512,256]{1,0:T(8,128)(2,1)} %cq_ref.1, bf16[1601,2,128]{2,1,0:T(2,128)(2,1)} %bitcast.7, s32[4,16]{1,0:T(4,128)} %seen_ref.1, s32[16]{0:T(128)} %owner_ref.1), custom_call_target="tpu_custom_call" | custom-call | flops 11264000000 | bytes 8000000 | tf_op jit(solution)/shard_map/pallas_call | solution.py:598
  111.3 1.9 %slice_bitcast_fusion = (bf16[512,256]{1,0:T(8,128)(2,1)}, bf16[512,256]{1,0:T(8,128)(2,1)}) fusion(bf16[2,512,256]{2,1,0:T(8,128)(2,1)} %shard_map.77), kind=kLoop, calls=%fused_computation | loop fusion | bytes 1048576 | tf_op jit(solution)/shard_map/squeeze | solution.py:652

commit v5 on v4

--- a/solution.py
+++ b/solution.py
@@ -104,8 +104,9 @@
 
     def text_unit(direction, distance, sem):
         chunk = 2 * layer(direction, distance) + y
+        rows = pl.ds(direction * BLOCK // 2, BLOCK // 2) if sem == 3 else pl.ds(0, BLOCK)
         return remote(
-            text.at[chunk], text.at[chunk],
+            text.at[chunk, rows], text.at[chunk, rows],
             tz_s.at[direction, sem], tz_r.at[direction, sem], onward(direction),
         )
 
@@ -118,12 +119,12 @@
 
     def text_event(distance):
         for direction in range(2):
-            if distance == 4 and direction == 1:
-                continue
             text_unit(direction, distance, distance - 1).wait_recv()
-            if distance < 3 or (distance == 3 and direction == 0):
+            if distance < 4:
                 text_unit(direction, distance, distance).start()
-            text_across(layer(direction, distance), y).start()
+                text_across(layer(direction, distance), y).start()
+        if distance == 4:
+            text_across(layer(0, 4), y).start()
 
     def peer(step):
         return (x + step) % ENC
@@ -559,8 +560,7 @@
     ring_sent(ring_b)
     for direction in range(2):
         for distance in range(4):
-            if distance < 3 or direction == 0:
-                text_unit(direction, distance, distance).wait_send()
+            text_unit(direction, distance, distance).wait_send()
     for k in range(LAYERS):
         text_across(k, y).wait_send()
     for which in range(2):

time: 114 us -> 114 us (level)
  no operation moved by 1% of the time
where the time goes in v5:
time: 114 us; the launch traced here: 113 us
  Pallas kernels  111 us (97%)
  local copies, waits for them, and re-layouts  1.85 us (2%)
    pallas_call x1, Pallas kernels, per_device(): pl.pallas_call(kernel, out_shape=jax.ShapeDtypeStruct((2, ROWS, 2 * HEAD)...  111 us

profile of v5, /device:TPU:16, one launch (start us, length us, event | category | flops | bytes accessed | tf_op | source)
XLA Modules:
  0.0 113.1 jit_solution(393546530509187745)
XLA Ops:
  0.6 110.6 %shard_map.77 = bf16[2,512,256]{2,1,0:T(8,128)(2,1)} custom-call(bf16[512,256]{1,0:T(8,128)(2,1)} %sq_ref.1, bf16[512,2,128]{2,1,0:T(2,128)(2,1)} %text_ref.1, bf16[512,256]{1,0:T(8,128)(2,1)} %cq_ref.1, bf16[1601,2,128]{2,1,0:T(2,128)(2,1)} %bitcast.7, s32[4,16]{1,0:T(4,128)} %seen_ref.1, s32[16]{0:T(128)} %owner_ref.1), custom_call_target="tpu_custom_call" | custom-call | flops 11264000000 | bytes 8000000 | tf_op jit(solution)/shard_map/pallas_call | solution.py:598
  111.2 1.9 %slice_bitcast_fusion = (bf16[512,256]{1,0:T(8,128)(2,1)}, bf16[512,256]{1,0:T(8,128)(2,1)}) fusion(bf16[2,512,256]{2,1,0:T(8,128)(2,1)} %shard_map.77), kind=kLoop, calls=%fused_computation | loop fusion | bytes 1048576 | tf_op jit(solution)/shard_map/squeeze | solution.py:652
